TPU v7x, 32 devices: a whole 2x2x4 slice. The times are simulated.
32 devices in a mesh: runs: 2 (over x), modes: 16 (over z, y, core).
Axes of the slice: x: 2, y: 2, z: 4, core: 2. Of those that a mesh axis runs over, the one named last changes fastest.
Arguments:
- amplitudes: float32 [8192, 2, 5, 512], P(('runs', 'modes')), parts along dimension 0, may hold values from -6 to 6
- mode_table: int32 [4096, 2], replicated, may hold values from 0 to 127, as said below
- slab_map: int32 [8], replicated, may hold values from 0 to 7, each once
- base_flow: float32 [1024], P('runs'), parts along dimension 0, may hold values from 0 to 1.5
- base_coupling: float32 [50, 512], P('runs'), parts along dimension 0, may hold values from -0.36 to 0.36
- slab_inverse: float32 [8, 64, 64], replicated
- wall_operator: float32 [64, 64], replicated, may hold values from -0.75 to 0.75
Outputs:
- marched: float32 [8192, 2, 5, 512], P(('runs', 'modes')), parts along dimension 0
There are 2 independent parts, one for each index of `runs`. A program takes and returns all parts, laid end to end along the dimension named above; an argument that names none is the same for every part. Nothing has to cross between parts.
Inputs may be any that keep to these rules, and one draw needn't show every extreme that they name: `mode_table`: every cell of the 32 x 128 grid is named by exactly one mode; column 0 lies in 0 to 31. `slab_map`: each subdomain has its own slot.
All inputs are finite; a program needn't handle non-finite values.
Results may differ from a plain program's by a relative error of at most 0.0003.
Values sent between devices are 32-bit elements; how exact they have to be, the bound alone decides.
A program may use at most 192 MiB of HBM per device.

v0:
```python
import math

import jax
import jax.numpy as jnp
from jax import lax
from jax.sharding import PartitionSpec as P

M = 4096
NB = 128
SWEEPS = 3
NW = 32


precise = lax.Precision.HIGHEST
omega_step = 0.01
phase_gain = 0.2
march_step = 0.2
coupling = 0.3


def twiddle(length):
    counter = jnp.arange(length, dtype=jnp.int32)
    product = counter[:, None] * counter[None, :] % length
    angles = product.astype(jnp.float32) * (2.0 * math.pi / length)
    return (jnp.cos(angles), jnp.sin(angles))


def mode_tables(mode_table):
    omega_index = mode_table[:, 0]
    beta_index = mode_table[:, 1]
    signed = jnp.where(beta_index >= NB // 2, beta_index - NB, beta_index)
    wavenum = 2.0 * signed.astype(jnp.float32) / NB
    frequency = omega_step * omega_index.astype(jnp.float32)
    grid_pos = omega_index * NB + beta_index
    mode_at = jnp.zeros((M,), jnp.int32).at[grid_pos].set(jnp.arange(M, dtype=jnp.int32))
    return (wavenum, frequency, grid_pos, mode_at)


def synthesize(real_part, imag_part, tables, factor):
    cos_omega, sin_omega, cos_beta, sin_beta = tables
    mixed_re = jnp.einsum("...wb,bz->...wz", real_part, cos_beta, precision=precise) - jnp.einsum(
        "...wb,bz->...wz", imag_part, sin_beta, precision=precise
    )
    mixed_im = jnp.einsum("...wb,bz->...wz", real_part, sin_beta, precision=precise) + jnp.einsum(
        "...wb,bz->...wz", imag_part, cos_beta, precision=precise
    )
    physical = jnp.einsum("...wz,wt->...tz", mixed_re, cos_omega, precision=precise) - jnp.einsum(
        "...wz,wt->...tz", mixed_im, sin_omega, precision=precise
    )
    return physical * factor


def analyze(physical, tables, factor):
    cos_omega, sin_omega, cos_beta, sin_beta = tables
    half_re = jnp.einsum("...tz,zb->...tb", physical, cos_beta, precision=precise)
    half_im = -jnp.einsum("...tz,zb->...tb", physical, sin_beta, precision=precise)
    coef_re = jnp.einsum("...tb,tw->...wb", half_re, cos_omega, precision=precise) + jnp.einsum(
        "...tb,tw->...wb", half_im, sin_omega, precision=precise
    )
    coef_im = jnp.einsum("...tb,tw->...wb", half_im, cos_omega, precision=precise) - jnp.einsum(
        "...tb,tw->...wb", half_re, sin_omega, precision=precise
    )
    return (coef_re * factor, coef_im * factor)


def forcing(normal_vel, spanwise_vel, wall_grad, span_grad, tables, factor):
    vel_v = synthesize(normal_vel[0], normal_vel[1], tables, factor)
    vel_w = synthesize(spanwise_vel[0], spanwise_vel[1], tables, factor)
    grad_y = synthesize(wall_grad[0], wall_grad[1], tables, factor)
    grad_z = synthesize(span_grad[0], span_grad[1], tables, factor)
    product = -(vel_v[None] * grad_y + vel_w[None] * grad_z)
    return analyze(product, tables, factor)


def wall_derivative(values, wall_operator):
    slab_width = wall_operator.shape[0]
    slab_count = values.shape[3] // slab_width
    blocks = values.reshape(values.shape[:3] + (slab_count, slab_width))
    return jnp.einsum("ij,abcsj->abcsi", wall_operator, blocks, precision=precise).reshape(
        values.shape
    )


def interface_table(slab_map, slab_count, slab_width):
    inverse = (
        jnp.zeros((slab_count,), jnp.int32)
        .at[slab_map]
        .set(jnp.arange(slab_count, dtype=jnp.int32))
    )
    position = jnp.arange(slab_count * slab_width, dtype=jnp.int32)
    slot_of = position // slab_width
    within = position % slab_width
    domain = inverse[slot_of]
    below = slab_map[jnp.maximum(domain - 1, 0)] * slab_width + (slab_width - 1)
    above = slab_map[jnp.minimum(domain + 1, slab_count - 1)] * slab_width
    lower_ok = (within == 0) & (domain > 0)
    upper_ok = (within == slab_width - 1) & (domain < slab_count - 1)
    source = jnp.where(lower_ok, below, jnp.where(upper_ok, above, 0))
    weight = (lower_ok | upper_ok).astype(jnp.float32)
    return (source, weight)


def relaxation(iterate, right_side, rotation, matrix, slab_inverse, source, weight):
    slab_count = slab_inverse.shape[0]
    slab_width = slab_inverse.shape[1]
    coupled = jnp.einsum("kjy,acjy->acky", matrix, iterate, precision=precise)
    applied = jnp.stack(
        [
            coupled[:, 0] - rotation[:, None, :] * iterate[:, 1],
            coupled[:, 1] + rotation[:, None, :] * iterate[:, 0],
        ],
        1,
    )
    rims = jnp.take(iterate, source, axis=3) * weight
    residual_in = right_side - applied + coupling * rims
    blocks = residual_in.reshape(iterate.shape[:3] + (slab_count, slab_width))
    return jnp.einsum("sij,acvsj->acvsi", slab_inverse, blocks, precision=precise).reshape(
        iterate.shape
    )


def local(amplitudes, mode_table, slab_map, base_flow, base_coupling, slab_inverse, wall_operator):
    local_modes = amplitudes.shape[0]
    wall_points = amplitudes.shape[3]
    groups = lax.axis_size("modes")
    point_share = wall_points // groups
    wavenum, frequency, grid_pos, mode_at = mode_tables(mode_table)
    first_mode = lax.axis_index("modes") * local_modes
    wave_local = lax.dynamic_slice_in_dim(wavenum, first_mode, local_modes)
    freq_local = lax.dynamic_slice_in_dim(frequency, first_mode, local_modes)
    tables = twiddle(NW) + twiddle(NB)
    factor = 1.0 / math.sqrt(M)
    source, weight = interface_table(slab_map, slab_inverse.shape[0], slab_inverse.shape[1])
    matrix = base_coupling.reshape(5, 5, wall_points)
    gradient = wall_derivative(amplitudes, wall_operator)
    span = jnp.stack(
        [
            -wave_local[:, None, None] * amplitudes[:, 1],
            wave_local[:, None, None] * amplitudes[:, 0],
        ],
        1,
    )
    fields = jnp.concatenate([amplitudes[:, :, 2:4], gradient, span], 2)
    field_count = fields.shape[2]
    channels = 2 * field_count
    outgoing = jnp.transpose(
        fields.reshape(local_modes, channels, groups, point_share), (1, 2, 3, 0)
    ).reshape(channels, groups, point_share * local_modes)
    incoming = lax.all_to_all(outgoing, "modes", split_axis=1, concat_axis=1, tiled=True)
    by_mode = jnp.transpose(
        incoming.reshape(channels, groups, point_share, local_modes), (0, 2, 1, 3)
    ).reshape(channels, point_share, M)
    gridded = by_mode[..., mode_at].reshape(2, field_count, point_share, NW, NB)
    normal_vel = gridded[:, 0]
    spanwise_vel = gridded[:, 1]
    wall_grad = gridded[:, 2:7]
    span_grad = gridded[:, 7:12]
    mean_crossflow = lax.all_gather(spanwise_vel[0, :, 0, 0], "modes", axis=0, tiled=True)
    coef_re, coef_im = forcing(normal_vel, spanwise_vel, wall_grad, span_grad, tables, factor)
    packed = jnp.stack([coef_re, coef_im], 0).reshape(10, point_share, M)[..., grid_pos]
    sendback = jnp.transpose(
        packed.reshape(10, point_share, groups, local_modes), (0, 2, 1, 3)
    ).reshape(10, groups, point_share * local_modes)
    returned = lax.all_to_all(sendback, "modes", split_axis=1, concat_axis=1, tiled=True)
    nonlinear = jnp.transpose(
        returned.reshape(10, groups, point_share, local_modes), (3, 0, 1, 2)
    ).reshape(local_modes, 2, 5, wall_points)
    crossflow = base_flow + mean_crossflow
    rotation = phase_gain * wave_local[:, None] * crossflow[None, :] - freq_local[:, None]
    right_side = amplitudes + march_step * nonlinear
    iterate = amplitudes
    for sweep_index in range(SWEEPS):
        iterate = relaxation(iterate, right_side, rotation, matrix, slab_inverse, source, weight)
    return iterate


def solution(mesh):
    return jax.shard_map(
        local,
        mesh=mesh,
        in_specs=(
            P(("runs", "modes"), None, None, None),
            P(),
            P(),
            P("runs"),
            P("runs", None),
            P(),
            P(),
        ),
        out_specs=P(("runs", "modes"), None, None, None),
        check_vma=False,
    )
```

profile of v0, /device:TPU:15, one launch (start us, length us, event | category | flops | bytes accessed | tf_op | source)
XLA Modules:
  0.0 1125.1 jit_solution(16035738039939335785)
XLA Ops:
  0.0 9.0 copy.115
  9.0 8.7 copy.102
  19.0 4.6 slice.154
  23.6 4.1 slice_multiply_fusion.5
  27.8 5.3 fusion.90
  36.3 7.8 maximum_maximum_fusion
  44.1 17.6 %copy.106 = f32[256,2,12,512]{0,3,2,1:T(8,128)} copy(f32[256,2,12,512]{0,2,1,3:T(8,128)} %maximum_maximum_fusion) | data formatting | bytes 25165824 | tf_op jit(solution)/shard_map/concatenate | solution.py:143
  61.7 14.2 %reshape.217 = f32[24,16,8192]{2,1,0:T(8,128)} reshape(f32[24,16,32,256]{3,2,1,0:T(8,128)} %bitcast.293) | data formatting | bytes 25165824 | tf_op jit(solution)/shard_map/reshape | solution.py:148
  75.9 16.4 %copy.107 = f32[24,16,8192]{2,0,1:T(8,128)} copy(f32[24,16,8192]{2,1,0:T(8,128)} %reshape.217) | data formatting | bytes 25165824 | tf_op jit(solution)/shard_map/reshape | solution.py:148
  92.3 6.6 all-to-all-start
  98.8 15.7 %scatter_custom_fusion = s32[4096]{0:T(1024)S(1)} fusion(s32[4096]{0:T(1024)S(1)} %bitcast.308, s32[4096]{0:T(1024)S(1)} %iota.30, s32[]{:T(128)} %constant.98.clone.1), kind=kCustom, calls=%fused_computation.165 | custom fusion | bytes 16388 | tf_op jit(solution)/shard_map/scatter | solution.py:35
  114.5 256.5 %all-to-all-done = f32[24,16,8192]{2,0,1:T(8,128)} async-done(((f32[24,16,8192]{2,0,1:T(8,128)}), f32[24,16,8192]{2,0,1:T(8,128)}, u32[]{:S(2)}, u32[]{:S(2)}) %all-to-all-start) | async-done | bytes 12582944 | tf_op jit(solution)/shard_map/all_to_all | solution.py:149
  371.0 14.6 %copy.146 = f32[48,8,32,256]{3,2,1,0:T(8,128)} copy(f32[48,8,32,256]{3,1,2,0:T(8,128)} %bitcast.101) | data formatting | bytes 25165824
  385.7 29.6 %copy.138 = f32[24,32,16,256]{1,0,3,2:T(8,128)} copy(f32[24,32,16,256]{3,1,0,2:T(8,128)} %bitcast.294) | data formatting | bytes 25165824 | tf_op jit(solution)/shard_map/reshape | solution.py:152
  415.3 86.4 %gather_fusion = f32[4096,24,32]{2,1,0:T(8,128)} fusion(f32[24,32,4096]{1,0,2:T(8,128)} %bitcast.291, s32[4096]{0:T(1024)S(1)} %fusion.115), kind=kCustom, calls=%fused_computation.3 | custom fusion | bytes 25182208 | tf_op jit(solution)/shard_map/gather | solution.py:153
  501.6 32.3 %copy.110 = f32[24,32,4096]{2,1,0:T(8,128)} copy(f32[24,32,4096]{1,0,2:T(8,128)} %bitcast.292) | data formatting | bytes 25165824 | tf_op jit(solution)/shard_map/gather | solution.py:153
  534.0 12.0 %copy.147 = f32[96,8,32,128]{3,2,1,0:T(8,128)} copy(f32[96,8,32,128]{3,1,2,0:T(8,128)} %bitcast.295) | data formatting | bytes 25165824
  554.1 4.3 fusion.26
  558.4 4.3 fusion.28
  592.5 3.5 fusion.17
  614.6 6.8 reshape.221
  621.5 22.0 %copy.111 = f32[10,32,4096]{1,0,2:T(8,128)} copy(f32[10,32,4096]{2,1,0:T(8,128)} %reshape.221) | data formatting | bytes 10485760 | tf_op jit(solution)/shard_map/reshape | solution.py:160
  643.5 78.3 %gather_fusion.1 = f32[4096,10,32]{2,1,0:T(8,128)} fusion(f32[10,32,4096]{1,0,2:T(8,128)} %copy.111, s32[4096]{0:T(1024)S(1)} %broadcast_clamp_fusion), kind=kCustom, calls=%fused_computation.4 | custom fusion | bytes 10502144 | tf_op jit(solution)/shard_map/gather | solution.py:160
  721.8 21.3 %copy.112 = f32[10,32,16,256]{3,1,2,0:T(8,128)} copy(f32[10,32,16,256]{1,0,3,2:T(8,128)} %bitcast.296) | data formatting | bytes 10485760 | tf_op jit(solution)/shard_map/reshape | solution.py:162
  743.1 6.9 reshape.223
  750.0 9.0 copy.113
  759.0 5.0 all-to-all-start.1
  765.4 4.4 compare_select_fusion.10
  771.2 4.4 compare_select_fusion.4
  775.6 5.8 compare_and_fusion
  781.4 7.8 gather_fusion.2
  791.9 11.8 %convolution_bitcast_fusion.2 = f32[256,2,5,512]{0,2,1,3:T(8,128)} fusion(f32[256,2,5,512]{0,2,1,3:T(8,128)} %copy.115, f32[5,5,512,1]{1,0,3,2:T(8,128)S(1)} %copy.134), kind=kOutput, calls=%fused_computation.43 | convolution fusion | flops 78643200 | bytes 10536960 | tf_op jit(solution)/shard_map/kjy,acjy->acky/dot_general | solution.py:106
  805.6 157.4 %all-reduce = f32[512]{0:T(512)S(1)} all-reduce(f32[512]{0:T(512)S(1)} %dynamic-update-slice), channel_id=2, replica_groups=mesh['runs'=2,'modes'=16] {'modes'}, use_global_device_ids=true, to_apply=%add | all-reduce | flops 512 | bytes 4096 | tf_op jit(solution)/shard_map/all_gather | solution.py:158
  964.0 10.0 slice_subtract_fusion
  973.9 6.8 copy_multiply_fusion
  985.5 11.0 fusion
  996.6 8.4 fusion.38
  1011.4 9.8 convolution_bitcast_fusion.1
  1021.2 7.8 gather_fusion.3
  1029.1 8.8 fusion.15
  1040.2 10.4 fusion.1
  1050.6 8.4 fusion.41
  1065.5 9.9 convolution_bitcast_fusion
  1075.4 7.9 gather_fusion.4
  1083.3 8.7 fusion.13
  1094.3 10.5 fusion.2
  1104.7 8.4 fusion.44
  1115.8 8.8 copy.128
  (110 shorter events, 93.7 us)
Async XLA Ops:
  0.0 996.6 %copy-start = (f32[8,64,64]{2,1,0:T(8,128)S(1)}, f32[8,64,64]{2,1,0:T(8,128)}, u32[]{:S(2)}) copy-start(f32[8,64,64]{2,1,0:T(8,128)} %param.14) | copy-start | bytes 393220
  9.0 8.7 copy-start.13
  19.0 8.8 slice-start.4
  23.6 4.1 slice-start.5
  23.6 4.1 copy-start.12
  92.3 278.8 %all-to-all-start = ((f32[24,16,8192]{2,0,1:T(8,128)}), f32[24,16,8192]{2,0,1:T(8,128)}, u32[]{:S(2)}, u32[]{:S(2)}) async-start(f32[24,16,8192]{2,0,1:T(8,128)} %copy.107), calls=%async_computation | async-start | bytes 25165824 | tf_op jit(solution)/shard_map/all_to_all | solution.py:149
  547.8 14.8 %copy-start.3 = (f32[96,8,32,128]{3,2,1,0:T(8,128)S(1)}, f32[96,8,32,128]{3,2,1,0:T(8,128)}, u32[]{:S(2)}) copy-start(f32[96,8,32,128]{3,2,1,0:T(8,128)} %copy.147) | copy-start | bytes 37748740
  759.0 5.0 copy-start.14
  759.0 214.9 %all-to-all-start.1 = ((f32[10,16,8192]{2,0,1:T(8,128)}), f32[10,16,8192]{2,0,1:T(8,128)}, u32[]{:S(2)}, u32[]{:S(2)}) async-start(f32[10,16,8192]{2,0,1:T(8,128)} %copy.113), calls=%async_computation.1 | async-start | bytes 16777216 | tf_op jit(solution)/shard_map/all_to_all | solution.py:164
  781.3 7.8 copy-start.11
  781.4 8.6 copy-start.17
  791.9 171.1 %copy-start.16 = (f32[512]{0:T(512)S(1)}, f32[512]{0:T(512)}, u32[]{:S(2)}) copy-start(f32[512]{0:T(512)} %param.12) | copy-start | bytes 6148
  791.9 171.1 %copy-start.15 = (f32[256]{0:T(256)S(1)}, f32[256]{0:T(256)}, u32[]{:S(2)}) copy-start(f32[256]{0:T(256)} %get-tuple-element.8) | copy-start | bytes 3076
  963.1 0.9 copy-start.9
  980.7 2.2 copy-start.7
  980.7 4.8 copy-start.8
  982.6 14.0 %copy-start.4 = (f32[20,8,32,256]{3,2,1,0:T(8,128)}, f32[20,8,32,256]{3,2,1,0:T(8,128)S(1)}, u32[]{:S(2)}) copy-start(f32[20,8,32,256]{3,2,1,0:T(8,128)S(1)} %copy.148) | copy-start | bytes 15728644
  1008.1 3.3 copy-start.2
  1021.2 16.6 %slice-start = ((s8[5242880]{0:T(1024)(128)(4,1)}), s8[1048576]{0:T(1024)(128)(4,1)S(1)}, s32[]{:S(2)}) async-start(s8[5242880]{0:T(1024)(128)(4,1)} %bitcast.285), calls=%async_computation.2 | async-start | bytes 2097152
  1029.1 8.8 slice-start.1
  1029.1 11.2 copy-start.6
  1062.2 3.3 copy-start.1
  1075.4 7.9 copy-start.10
  1075.4 16.6 %slice-start.2 = ((s8[5242880]{0:T(1024)(128)(4,1)}), s8[1048576]{0:T(1024)(128)(4,1)S(1)}, s32[]{:S(2)}) async-start(s8[5242880]{0:T(1024)(128)(4,1)} %bitcast.288), calls=%async_computation.4 | async-start | bytes 2097152
  1083.2 8.7 slice-start.3
  1083.3 11.0 copy-start.5
where the time goes:
time: 1140 us; the launch traced here: 1130 us
  local copies, waits for them, and re-layouts  472 us (41%)
  waiting for transfers between devices  256 us (22%)
  blocking collectives  157 us (14%)
  matrix products  127 us (11%)
  other arithmetic  98.3 us (9%)
  starting transfers between devices  11.6 us (1%)
    all_to_all x1, waiting for transfers between devices, local(): lax.all_to_all(outgoing, 'modes', split_axis=1, concat_axis=1, tiled=True)  256 us
    all_gather x1, blocking collectives, local(): lax.all_gather(spanwise_vel[0, :, 0, 0], 'modes', axis=0, tiled=True)  157 us
    gather x2, local copies, waits for them, and re-layouts, local(): gridded = by_mode[..., mode_at].reshape(2, field_count, point_share, NW, NB)  119 us
    gather x1, local copies, waits for them, and re-layouts, local(): jnp.stack([coef_re, coef_im], 0).reshape(10, point_share, M)[..., grid_pos]  78.3 us
    unnamed x56, local copies, waits for them, and re-layouts  62 us
    add x3, other arithmetic, relaxation(): residual_in = right_side - applied + coupling * rims  31.9 us
    dot_general x3, matrix products, relaxation(): coupled = jnp.einsum('kjy,acjy->acky', matrix, iterate, precision=precise)  31.5 us
    reshape x2, local copies, waits for them, and re-layouts, local(): outgoing = jnp.transpose(fields.reshape(local_modes, channels, groups, po...  30.6 us
  transfers between devices with their start and end apart: 2, of which 1 were waited for; matrix products, arithmetic and copies ran while one was open for 6% of the time, Pallas kernels for 0%

commit v1 on v0

--- a/solution.py
+++ b/solution.py
@@ -2,7 +2,11 @@
 
 import jax
 import jax.numpy as jnp
+import ml_dtypes
+import numpy as np
 from jax import lax
+from jax.experimental import pallas as pl
+from jax.experimental.pallas import tpu as pltpu
 from jax.sharding import PartitionSpec as P
 
 M = 4096
@@ -174,9 +178,507 @@
     return iterate
 
 
+F32 = jnp.float32
+BF16 = jnp.bfloat16
+VMEM_BYTES = 56 * 1024 * 1024
+SHARE = 32
+LANES = 128
+
+
+def split_np(values):
+    high = values.astype(np.float32).astype(ml_dtypes.bfloat16)
+    low = (values - high.astype(np.float64)).astype(np.float32).astype(ml_dtypes.bfloat16)
+    return high, low
+
+
+def split(values):
+    high = values.astype(BF16)
+    low = (values - high.astype(F32)).astype(BF16)
+    return high, low
+
+
+def dot(left, right):
+    return jnp.dot(left, right, preferred_element_type=F32)
+
+
+def dot3(left, right):
+    return dot(left[0], right[0]) + (dot(left[0], right[1]) + dot(left[1], right[0]))
+
+
+def synthesis_matrix():
+    index = np.arange(NB)
+    angle = 2.0 * np.pi * (index[:, None] * index[None, :] % NB) / NB
+    cos, sin = np.cos(angle), np.sin(angle)
+    signed = np.where(index >= NB // 2, index - NB, index)
+    wave = (2.0 * signed / NB)[None, :]
+    rows = [
+        np.concatenate([cos, -sin], 1),
+        np.concatenate([sin, cos], 1),
+        np.concatenate([-sin * wave, -cos * wave], 1),
+        np.concatenate([cos * wave, -sin * wave], 1),
+    ]
+    return np.concatenate(rows, 0) / math.sqrt(M)
+
+
+def analysis_matrix():
+    index = np.arange(NB)
+    angle = 2.0 * np.pi * (index[:, None] * index[None, :] % NB) / NB
+    cos, sin = np.cos(angle), np.sin(angle)
+    rows = [np.concatenate([cos, sin], 1), np.concatenate([-sin, cos], 1)]
+    return np.concatenate(rows, 0) / math.sqrt(M)
+
+
+def weighted(terms, weights):
+    total = None
+    for term, weight in zip(terms, weights):
+        if abs(weight) < 1e-12:
+            continue
+        if abs(weight - 1.0) < 1e-12:
+            part = term
+        elif abs(weight + 1.0) < 1e-12:
+            part = -term
+        else:
+            part = term * np.float32(weight)
+        total = part if total is None else total + part
+    return total
+
+
+def cosine_sums(terms):
+    half, quarter = NW // 2, NW // 4
+    out = [None] * (half + 1)
+    for t in range(quarter + 1):
+        even = weighted(terms[0::2], [math.cos(2 * math.pi * w * t / NW) for w in range(0, half + 1, 2)])
+        odd = weighted(terms[1::2], [math.cos(2 * math.pi * w * t / NW) for w in range(1, half + 1, 2)])
+        if odd is None:
+            out[t] = even
+            out[half - t] = even
+        else:
+            out[t] = even + odd
+            out[half - t] = even - odd
+    return out
+
+
+def sine_sums(terms):
+    half, quarter = NW // 2, NW // 4
+    out = [None] * half
+    for t in range(1, quarter + 1):
+        even = weighted(terms[2::2], [math.sin(2 * math.pi * w * t / NW) for w in range(2, half, 2)])
+        odd = weighted(terms[1::2], [math.sin(2 * math.pi * w * t / NW) for w in range(1, half, 2)])
+        if even is None:
+            out[t] = odd
+        else:
+            out[t] = odd + even
+            out[half - t] = odd - even
+    return out
+
+
+def lane_group(shape):
+    return lax.broadcasted_iota(jnp.int32, shape, len(shape) - 1) // SHARE
+
+
+def shifted(values, groups):
+    groups = groups % 4
+    return values if groups == 0 else pltpu.roll(values, groups * SHARE, values.ndim - 1)
+
+
+def join(pieces, which):
+    low = jnp.where(which == 0, pieces[0], pieces[1])
+    high = jnp.where(which == 2, pieces[2], pieces[3])
+    return jnp.where(which < 2, low, high)
+
+
+def pack_kernel(amp_ref, out_ref):
+    half = amp_ref.shape[1] // 2
+    full = 2 * half
+    which = lane_group((8, LANES))
+
+    def body(step, carry):
+        row = pl.multiple_of(step * 8, 8)
+        for tile in range(4):
+            lanes = pl.ds(tile * LANES, LANES)
+            rims = []
+            for side in range(2):
+                rows = pl.ds(row + side * half, 8)
+                parts = [amp_ref[c, rows, lanes] for c in range(10)]
+                rims += [parts[4], parts[9]]
+                for q in range(4):
+                    dest = tile * 4 + q
+                    for block, first in ((0, 0), (1, 5)):
+                        out_ref[dest, pl.ds(row + side * half + block * full, 8), :] = join(
+                            [shifted(parts[first + k], k - q) for k in range(4)], which
+                        )
+            for q in range(4):
+                out_ref[tile * 4 + q, pl.ds(row + 2 * full, 8), :] = join(
+                    [shifted(rims[k], k - q) for k in range(4)], which
+                )
+        return carry
+
+    lax.fori_loop(0, half // 8, body, 0)
+
+
+def physical_kernel(pos_ref, in_ref, high_ref, low_ref, field_ref, span_ref, mean_ref, ga, gb, gc, mid):
+    sources = in_ref.shape[0]
+    half = M // sources // 2
+    full = 2 * half
+
+    def spread(source, carry):
+        def rows_of(step, inner):
+            row = pl.multiple_of(step * 8, 8)
+            rest = in_ref[source, pl.ds(row + 2 * full, 8), :]
+            for side in range(2):
+                first = row + side * half
+                a8 = in_ref[source, pl.ds(first, 8), :]
+                b8 = in_ref[source, pl.ds(first + full, 8), :]
+                c8 = shifted(rest, 2 * side)
+                for u in range(8):
+                    where = pos_ref[source * full + first + u]
+                    ga[pl.ds(where, 1), :] = a8[u : u + 1, :]
+                    gb[pl.ds(where, 1), :] = b8[u : u + 1, :]
+                    gc[pl.ds(where, 1), :] = c8[u : u + 1, :]
+            return inner
+
+        return lax.fori_loop(0, half // 8, rows_of, carry)
+
+    lax.fori_loop(0, sources, spread, 0)
+    mean_ref[...] = jnp.broadcast_to(ga[0:1, :], mean_ref.shape)
+
+    first_group = lane_group((NB, LANES)) == 0
+
+    def beta_sum(omega, carry):
+        rows = pl.ds(pl.multiple_of(omega * NB, NB), NB)
+        rest = gc[rows, :]
+        data = jnp.concatenate(
+            [
+                jnp.concatenate([ga[rows, :], rest], 1),
+                jnp.concatenate([gb[rows, :], shifted(rest, 3)], 1),
+            ],
+            0,
+        )
+        out = dot3((high_ref[...], low_ref[...]), split(data))
+        mid[omega, 0 : 4 * NB, :] = out[:, :LANES]
+        tail = out[:, LANES:]
+        for part in range(2):
+            mid[omega, (4 + part) * NB : (5 + part) * NB, :] = jnp.where(
+                first_group,
+                tail[part * NB : (part + 1) * NB],
+                shifted(tail[(2 + part) * NB : (3 + part) * NB], 1),
+            )
+        return carry
+
+    lax.fori_loop(0, NW, beta_sum, 0)
+
+    which = lane_group((8, LANES))
+
+    def omega_sum(step, carry):
+        row = pl.multiple_of(step * 8, 8)
+        for group in range(3):
+            re = [mid[w, pl.ds(row + 2 * group * NB, 8), :] for w in range(NW)]
+            im = [mid[w, pl.ds(row + (2 * group + 1) * NB, 8), :] for w in range(NW)]
+            half_w = NW // 2
+            cos_terms = [re[0]] + [re[w] + re[NW - w] for w in range(1, half_w)] + [re[half_w]]
+            sin_terms = [None] + [im[w] - im[NW - w] for w in range(1, half_w)]
+            even = cosine_sums(cos_terms)
+            odd = sine_sums(sin_terms)
+            out = [None] * NW
+            out[0] = even[0]
+            out[half_w] = even[half_w]
+            for t in range(1, half_w):
+                out[t] = even[t] - odd[t]
+                out[NW - t] = even[t] + odd[t]
+            if group < 2:
+                target = (field_ref, span_ref)[group]
+                for t in range(NW):
+                    target[t, pl.ds(row, 8), :] = out[t]
+            else:
+                for t in range(8):
+                    for target, start in ((field_ref, 0), (span_ref, 1)):
+                        target[NW + t, pl.ds(row, 8), :] = join(
+                            [shifted(out[t + 8 * k], k - start) for k in range(4)], which
+                        )
+        return carry
+
+    lax.fori_loop(0, NB // 8, omega_sum, 0)
+
+
+def force_kernel(
+    pos_ref, field_ref, other_ref, span_ref, mean_ref, wall_ref, high_ref, low_ref, out_ref,
+    force, mid, na, nb, nc, rest_rows,
+):
+    sources = out_ref.shape[0]
+    half = M // sources // 2
+    full = 2 * half
+    wall = split(wall_ref[...])
+
+    def products(step, carry):
+        which = lane_group((NB, LANES))
+
+        def gradient(row):
+            both = jnp.concatenate([field_ref[row], other_ref[row]], 1)
+            return dot3(split(both), wall)
+
+        packed_v = packed_w = None
+        for k in range(4):
+            t = step + 8 * k
+            own = field_ref[t]
+            v = join([shifted(own, j - 2) for j in range(4)], which)
+            w = join([shifted(own, j - 3) for j in range(4)], which)
+            force[t] = -(v * gradient(t) + w * span_ref[t])
+            packed_v = v if k == 0 else jnp.where(which == k, v, packed_v)
+            packed_w = w if k == 0 else jnp.where(which == k, w, packed_w)
+        t = step + NW
+        force[t] = -(packed_v * gradient(t) + packed_w * span_ref[t])
+        return carry
+
+    lax.fori_loop(0, 8, products, 0)
+
+    half_w = NW // 2
+
+    def time_sum(step, carry):
+        row = pl.multiple_of(step * 8, 8)
+        rows = pl.ds(row, 8)
+        for group in range(2):
+            if group == 0:
+                values = [force[t, rows, :] for t in range(NW)]
+            else:
+                packed = [force[NW + t, rows, :] for t in range(8)]
+                values = [shifted(packed[t % 8], -(t // 8)) for t in range(NW)]
+            cos_terms = (
+                [values[0]]
+                + [values[t] + values[NW - t] for t in range(1, half_w)]
+                + [values[half_w]]
+            )
+            sin_terms = [None] + [values[NW - t] - values[t] for t in range(1, half_w)]
+            even = cosine_sums(cos_terms)
+            odd = sine_sums(sin_terms)
+            lanes = slice(group * LANES, (group + 1) * LANES)
+            zero = jnp.zeros((8, LANES), F32)
+            for w in range(half_w + 1):
+                mid[w, rows, lanes] = even[w]
+                mid[w, pl.ds(row + NB, 8), lanes] = odd[w] if 0 < w < half_w else zero
+        return carry
+
+    lax.fori_loop(0, NB // 8, time_sum, 0)
+
+    first_group = lane_group((NB, LANES)) == 0
+
+    def span_sum(omega, carry):
+        out = dot3((high_ref[...], low_ref[...]), split(mid[omega]))
+        rows = pl.ds(pl.multiple_of(omega * NB, NB), NB)
+        na[rows, :] = out[:NB, :LANES]
+        nb[rows, :] = out[NB:, :LANES]
+        nc[rows, :] = jnp.where(first_group, out[:NB, LANES:], shifted(out[NB:, LANES:], 1))
+        return carry
+
+    lax.fori_loop(0, half_w + 1, span_sum, 0)
+
+    which = lane_group((8, LANES))
+
+    def collect(source, carry):
+        def rows_of(step, inner):
+            row = pl.multiple_of(step * 8, 8)
+            for side in range(2):
+                first = row + side * half
+                for u in range(8):
+                    where = pos_ref[source * full + first + u]
+                    out_ref[source, pl.ds(first + u, 1), :] = na[pl.ds(where, 1), :]
+                    out_ref[source, pl.ds(first + full + u, 1), :] = nb[pl.ds(where, 1), :]
+                    rest_rows[side, pl.ds(row + u, 1), :] = nc[pl.ds(where, 1), :]
+            return inner
+
+        lax.fori_loop(0, half // 8, rows_of, 0)
+        wide = lane_group((half, LANES)) < 2
+        out_ref[source, 2 * full : 2 * full + half, :] = jnp.where(
+            wide, rest_rows[0], shifted(rest_rows[1], 2)
+        )
+        out_ref[source, 2 * full + half : 2 * full + half + 8, :] = mean_ref[...]
+        return carry
+
+    lax.fori_loop(0, sources, collect, 0)
+
+
+def sweep_kernel(
+    amp_ref, back_ref, base_ref, matrix_ref, inverse_ref, rim_ref, wave_ref, freq_ref, sign_ref,
+    out_ref, right, current, residual, flow,
+):
+    half = amp_ref.shape[1] // 2
+    full = 2 * half
+    rows_in = 16
+    which = lane_group((rows_in, LANES))
+    which8 = lane_group((8, LANES))
+    for tile in range(4):
+        mean = join(
+            [shifted(back_ref[4 * tile + k, 2 * full + half : 2 * full + half + 8, :], k - 3) for k in range(4)],
+            which8,
+        )
+        flow[:, tile * LANES : (tile + 1) * LANES] = mean + base_ref[:, tile * LANES : (tile + 1) * LANES]
+    inverse = [split(inverse_ref[g]) for g in range(2)]
+
+    def chunk(step, carry):
+        row = pl.multiple_of(step * rows_in, rows_in)
+        for tile in range(4):
+            lanes = slice(tile * LANES, (tile + 1) * LANES)
+            rest = [back_ref[4 * tile + k, pl.ds(row + 2 * full, rows_in), :] for k in range(4)]
+            for side in range(2):
+                rows = pl.ds(row + side * half, rows_in)
+                sign = sign_ref[rows, :]
+                for part in range(2):
+                    got = [
+                        back_ref[4 * tile + k, pl.ds(row + side * half + part * full, rows_in), :]
+                        for k in range(4)
+                    ]
+                    for c in range(5):
+                        if c < 4:
+                            value = join([shifted(got[k], k - c) for k in range(4)], which)
+                        else:
+                            value = join([shifted(rest[k], k - 2 * side - part) for k in range(4)], which)
+                        if part == 1:
+                            value = value * sign
+                        own = amp_ref[5 * part + c, rows, lanes]
+                        place = slice((5 * part + c) * 32 + side * 16, (5 * part + c) * 32 + side * 16 + 16)
+                        current[place, lanes] = own
+                        right[place, lanes] = own + march_step * value
+
+        for sweep in range(SWEEPS):
+            high, low = split(current[...])
+            residual[...] = right[...] + coupling * (dot(high, rim_ref[...]) + dot(low, rim_ref[...]))
+            for tile in range(4):
+                lanes = slice(tile * LANES, (tile + 1) * LANES)
+                for side in range(2):
+                    rows = pl.ds(row + side * half, rows_in)
+                    rotation = phase_gain * wave_ref[rows, :] * flow[0:1, lanes] - freq_ref[rows, :]
+                    x = [current[c * 32 + side * 16 : c * 32 + side * 16 + 16, lanes] for c in range(10)]
+                    for part in range(2):
+                        for c in range(5):
+                            total = rotation * x[5 * (1 - part) + c]
+                            if part == 0:
+                                total = -total
+                            for j in range(5):
+                                total = total + matrix_ref[5 * c + j : 5 * c + j + 1, lanes] * x[5 * part + j]
+                            place = slice((5 * part + c) * 32 + side * 16, (5 * part + c) * 32 + side * 16 + 16)
+                            residual[place, lanes] = residual[place, lanes] - total
+            for g in range(2):
+                lanes = slice(g * 256, (g + 1) * 256)
+                current[:, lanes] = dot3(split(residual[:, lanes]), inverse[g])
+        for c in range(10):
+            for side in range(2):
+                out_ref[c, pl.ds(row + side * half, rows_in), :] = current[
+                    c * 32 + side * 16 : c * 32 + side * 16 + 16, :
+                ]
+        return carry
+
+    lax.fori_loop(0, half // rows_in, chunk, 0)
+
+
+def local_fast(amplitudes, mode_table, slab_map, base_flow, base_coupling, slab_inverse, wall_operator):
+    local_modes = amplitudes.shape[0]
+    points = amplitudes.shape[3]
+    groups = lax.axis_size("modes")
+    me = lax.axis_index("modes")
+    half = local_modes // 2
+    vmem = pl.BlockSpec(memory_space=pltpu.VMEM)
+    smem = pl.BlockSpec(memory_space=pltpu.SMEM)
+    params = pltpu.CompilerParams(vmem_limit_bytes=VMEM_BYTES)
+    width = slab_inverse.shape[1]
+
+    omega_index = mode_table[:, 0]
+    beta_index = mode_table[:, 1]
+    grid_pos = omega_index * NB + beta_index
+    mirrored = omega_index > NW // 2
+    back_pos = jnp.where(mirrored, (NW - omega_index) * NB + (NB - beta_index) % NB, grid_pos)
+    local_table = lax.dynamic_slice_in_dim(mode_table, me * local_modes, local_modes)
+    omega_local = local_table[:, 0:1]
+    beta_local = local_table[:, 1:2]
+    signed = jnp.where(beta_local >= NB // 2, beta_local - NB, beta_local)
+    wave_local = 2.0 * signed.astype(F32) / NB
+    freq_local = omega_step * omega_local.astype(F32)
+    sign_local = jnp.where(omega_local > NW // 2, -1.0, 1.0).astype(F32)
+
+    part = lax.rem(me, 2) * SHARE
+    rows = lax.dynamic_slice_in_dim(wall_operator, part, SHARE, 0)
+    mine = lax.dynamic_slice_in_dim(rows, part, SHARE, 1)
+    theirs = lax.dynamic_slice_in_dim(rows, SHARE - part, SHARE, 1)
+    eye = jnp.eye(4, dtype=F32)
+
+    def blocks(value):
+        size = value.shape[0]
+        return (eye[:, None, :, None] * value.T[None, :, None, :]).reshape(4 * size, 4 * size)
+
+    wall = jnp.concatenate([blocks(mine), blocks(theirs)], 0)
+    turned = jnp.swapaxes(slab_inverse, 1, 2).reshape(2, 4, width, 1, width)
+    inverse = (turned * eye[None, :, None, :, None]).reshape(2, 4 * width, 4 * width)
+    source, weight = interface_table(slab_map, slab_inverse.shape[0], width)
+    rim = ((jnp.arange(points, dtype=jnp.int32)[:, None] == source[None, :]) & (weight[None, :] > 0)).astype(BF16)
+
+    amp = jnp.transpose(amplitudes, (1, 2, 0, 3)).reshape(10, local_modes, points)
+    message = pl.pallas_call(
+        pack_kernel,
+        out_shape=jax.ShapeDtypeStruct((groups, 5 * half, LANES), F32),
+        in_specs=[vmem],
+        out_specs=vmem,
+        compiler_params=params,
+        name="pack",
+    )(amp)
+    arrived = lax.all_to_all(message, "modes", split_axis=0, concat_axis=0, tiled=True)
+
+    high, low = split_np(synthesis_matrix())
+    block = jax.ShapeDtypeStruct((NW + 8, NB, LANES), F32)
+    field, span, mean = pl.pallas_call(
+        physical_kernel,
+        out_shape=[block, block, jax.ShapeDtypeStruct((8, LANES), F32)],
+        in_specs=[smem, vmem, vmem, vmem],
+        out_specs=[vmem, vmem, vmem],
+        scratch_shapes=[pltpu.VMEM((M, LANES), F32)] * 3 + [pltpu.VMEM((NW, 6 * NB, LANES), F32)],
+        compiler_params=params,
+        name="physical",
+    )(grid_pos, arrived, jnp.asarray(high), jnp.asarray(low))
+    other = lax.ppermute(field, "modes", [(i, i ^ 1) for i in range(groups)])
+
+    high, low = split_np(analysis_matrix())
+    rows_back = (NW // 2 + 1) * NB
+    sendback = pl.pallas_call(
+        force_kernel,
+        out_shape=jax.ShapeDtypeStruct((groups, 5 * half + 8, LANES), F32),
+        in_specs=[smem] + [vmem] * 7,
+        out_specs=vmem,
+        scratch_shapes=[
+            pltpu.VMEM((NW + 8, NB, LANES), F32),
+            pltpu.VMEM((NW // 2 + 1, 2 * NB, 2 * LANES), F32),
+        ]
+        + [pltpu.VMEM((rows_back, LANES), F32)] * 3
+        + [pltpu.VMEM((2, half, LANES), F32)],
+        compiler_params=params,
+        name="force",
+    )(back_pos, field, other, span, mean, wall, jnp.asarray(high), jnp.asarray(low))
+    returned = lax.all_to_all(sendback, "modes", split_axis=0, concat_axis=0, tiled=True)
+
+    marched = pl.pallas_call(
+        sweep_kernel,
+        out_shape=jax.ShapeDtypeStruct((10, local_modes, points), F32),
+        in_specs=[vmem] * 9,
+        out_specs=vmem,
+        scratch_shapes=[pltpu.VMEM((320, points), F32)] * 3 + [pltpu.VMEM((8, points), F32)],
+        compiler_params=params,
+        name="sweeps",
+    )(amp, returned, base_flow[None, :], base_coupling, inverse, rim, wave_local, freq_local, sign_local)
+    return jnp.transpose(marched.reshape(2, 5, local_modes, points), (2, 0, 1, 3))
+
+
+def run(amplitudes, mode_table, slab_map, base_flow, base_coupling, slab_inverse, wall_operator):
+    groups = lax.axis_size("modes")
+    fits = (
+        amplitudes.shape == (256, 2, 5, 512)
+        and groups * SHARE == amplitudes.shape[3]
+        and slab_inverse.shape == (8, 2 * SHARE, 2 * SHARE)
+    )
+    chosen = local_fast if fits else local
+    return chosen(
+        amplitudes, mode_table, slab_map, base_flow, base_coupling, slab_inverse, wall_operator
+    )
+
+
 def solution(mesh):
     return jax.shard_map(
-        local,
+        run,
         mesh=mesh,
         in_specs=(
             P(("runs", "modes"), None, None, None),

time: 1140 us -> 375 us (0.33); the launches traced: 1130 us -> 375 us
  local copies, waits for them, and re-layouts: 472 us -> 20.8 us
  blocking collectives: 157 us -> 0 us
  matrix products: 127 us -> 0 us
  Pallas kernels: 0 us -> 110 us
  other arithmetic: 98.3 us -> 20.4 us
  waiting for transfers between devices: 256 us -> 211 us
    gather x6 -> x0, local copies, waits for them, and re-layouts: 221 us -> none  [the longest x2 119 us: local(): gridded = by_mode[..., mode_at].reshape(2, field_count, point_share, NW, NB)]
    all_gather x1 -> x0, blocking collectives: 157 us -> none  [local(): lax.all_gather(spanwise_vel[0, :, 0, 0], 'modes', axis=0, tiled=True)]
    reshape x12 -> x1, local copies, waits for them, and re-layouts: 139 us -> 8.89 us  [local_fast(): marched.reshape(2, 5, local_modes, points)]
    dot_general x37 -> x0, matrix products: 127 us -> none  [the longest x3 31.5 us: relaxation(): coupled = jnp.einsum('kjy,acjy->acky', matrix, iterate, precision=precise)]
    pallas_call x0 -> x4, Pallas kernels: none -> 110 us  [the longest x1 43.7 us: local_fast(): pl.pallas_call(physical_kernel, out_shape=[block, block, jax.ShapeDtypeSt...]
    unnamed x56 -> x14, local copies, waits for them, and re-layouts: 62 us -> 1.85 us
    all_to_all x2, waiting for transfers between devices: 256 us -> 208 us  [the longest x1 114 us: local_fast(): lax.all_to_all(message, 'modes', split_axis=0, concat_axis=0, tiled=True)]
    add x4 -> x0, other arithmetic: 31.9 us -> none  [the longest x3 31.9 us: relaxation(): residual_in = right_side - applied + coupling * rims]
  transfers between devices with their start and end apart: 2 -> 3, of which waited for: 1 -> 3; matrix products, arithmetic and copies ran while one was open for 6% -> 7% of each run, Pallas kernels for 0% -> 0%
where the time goes in v1:
time: 375 us
  waiting for transfers between devices  211 us (56%)
  Pallas kernels  110 us (29%)
  local copies, waits for them, and re-layouts  20.8 us (6%)
  other arithmetic  20.4 us (5%)
  starting transfers between devices  11.9 us (3%)
    all_to_all x1, waiting for transfers between devices, local_fast(): lax.all_to_all(message, 'modes', split_axis=0, concat_axis=0, tiled=True)  114 us
    all_to_all x1, waiting for transfers between devices, local_fast(): lax.all_to_all(sendback, 'modes', split_axis=0, concat_axis=0, tiled=True)  94 us
    pallas_call x1, Pallas kernels, local_fast(): pl.pallas_call(physical_kernel, out_shape=[block, block, jax.ShapeDtypeSt...  43.7 us
    pallas_call x1, Pallas kernels, local_fast(): pl.pallas_call(sweep_kernel, out_shape=jax.ShapeDtypeStruct((10, local_mo...  29.5 us
    pallas_call x1, Pallas kernels, local_fast(): pl.pallas_call(force_kernel, out_shape=jax.ShapeDtypeStruct((groups, 5 *...  27.1 us
    pallas_call x1, Pallas kernels, local_fast(): pl.pallas_call(pack_kernel, out_shape=jax.ShapeDtypeStruct((groups, 5 * h...  9.96 us
    reshape x1, local copies, waits for them, and re-layouts, local_fast(): marched.reshape(2, 5, local_modes, points)  8.89 us
  transfers between devices with their start and end apart: 3, of which 3 were waited for; matrix products, arithmetic and copies ran while one was open for 7% of the time, Pallas kernels for 0%

profile of v1, /device:TPU:15, one launch (start us, length us, event | category | flops | bytes accessed | tf_op | source)
XLA Modules:
  0.0 374.7 jit_solution(12075706097999431064)
XLA Ops:
  0.0 5.9 %copy.18 = f32[2,5,256,512]{3,2,1,0:T(8,128)} copy(f32[2,5,256,512]{3,0,1,2:T(2,128)} %bitcast.39) | data formatting | bytes 10485760 | tf_op jit(solution)/shard_map/transpose | solution.py:612
  5.9 10.0 %pack.1 = f32[16,640,128]{2,1,0:T(8,128)} custom-call(f32[10,256,512]{2,1,0:T(8,128)} %bitcast.36), custom_call_target="tpu_custom_call" | custom-call | tf_op jit(solution)/shard_map/pack/pallas_call | solution.py:613
  15.8 6.7 %all-to-all-start = ((f32[16,640,128]{2,1,0:T(8,128)}), f32[16,640,128]{2,1,0:T(8,128)}, u32[]{:S(2)}, u32[]{:S(2)}) async-start(f32[16,640,128]{2,1,0:T(8,128)} %pack.1), calls=%async_computation | async-start | bytes 10485760 | tf_op jit(solution)/shard_map/all_to_all | solution.py:621
  22.5 0.0 copy-done.3
  22.5 0.0 copy-start.4
  22.5 0.6 slice_subtract_fusion
  23.2 114.3 %all-to-all-done.in_ref = f32[16,640,128]{2,1,0:T(8,128)} async-done(((f32[16,640,128]{2,1,0:T(8,128)}), f32[16,640,128]{2,1,0:T(8,128)}, u32[]{:S(2)}, u32[]{:S(2)}) %all-to-all-start) | async-done | bytes 5242912 | tf_op jit(solution)/shard_map/all_to_all | solution.py:621
  137.4 43.7 %physical.1 = (f32[40,128,128]{2,1,0:T(8,128)}, f32[40,128,128]{2,1,0:T(8,128)}, f32[8,128]{1,0:T(8,128)}) custom-call(s32[4096]{0:T(1024)} %bitcast.41, f32[16,640,128]{2,1,0:T(8,128)} %all-to-all-done.in_ref, bf16[512,256]{1,0:T(8,128)(2,1)} %constant.123.clone.high_ref, bf16[512,256]{1,0:T(8,128)(2,1)} %constant.124.clone.low_ref), custom_call_target="tpu_custom_call" | custom-call | tf_op jit(solution)/shard_map/physical/pallas_call | solution.py:625
  181.2 0.2 collective-permute-start
  181.4 0.0 copy-done.4
  181.4 0.1 dynamic-slice_bitcast_fusion.1
  181.4 0.1 copy.19
  181.5 0.1 copy.20
  181.6 0.1 broadcast_multiply_fusion.2
  181.7 0.2 mul.101
  181.9 0.2 mul.104
  182.1 0.1 compare_reduce_fusion
  182.1 0.7 pad_maximum_fusion.wall_ref
  182.8 0.0 copy-done.2
  182.8 0.6 fusion.6.pos_ref
  183.4 2.9 collective-permute-done.other_ref
  186.3 1.5 copy-done
  187.8 27.1 %force.1 = f32[16,648,128]{2,1,0:T(8,128)} custom-call(s32[4096]{0:T(1024)} %fusion.6.pos_ref, f32[40,128,128]{2,1,0:T(8,128)} %get-tuple-element.8.field_ref, f32[40,128,128]{2,1,0:T(8,128)} %copy-done, f32[40,128,128]{2,1,0:T(8,128)} %get-tuple-element.9.span_ref, f32[8,128]{1,0:T(8,128)} %get-tuple-element.10.mean_ref, ...), custom_call_target="tpu_custom_call" | custom-call | tf_op jit(solution)/shard_map/force/pallas_call | solution.py:638
  214.9 5.0 %all-to-all-start.1 = ((f32[16,648,128]{2,1,0:T(8,128)}), f32[16,648,128]{2,1,0:T(8,128)}, u32[]{:S(2)}, u32[]{:S(2)}) async-start(f32[16,648,128]{2,1,0:T(8,128)} %force.1), calls=%async_computation.1 | async-start | bytes 10616832 | tf_op jit(solution)/shard_map/all_to_all | solution.py:652
  219.9 0.1 constant_dynamic-slice_fusion
  220.0 0.1 copy.25
  220.1 0.1 copy.26
  220.3 0.1 mul.108
  220.4 0.3 mul.109
  220.8 0.0 copy-done.1
  220.8 0.1 copy.21
  220.9 0.2 mul.106
  221.1 0.6 mul.107
  221.7 0.0 copy-done.5
  221.8 0.8 scatter_custom_fusion
  222.6 0.7 fusion.23
  223.3 4.3 %compare_select_fusion.10 = s32[512,1]{0,1:T(1,128)S(1)} fusion(s32[]{:T(128)} %bitcast.11, s32[]{:T(128)} %bitcast.12, s32[]{:T(128)} %bitcast.13, s32[]{:T(128)} %bitcast.14, s32[]{:T(128)} %bitcast.15, s32[]{:T(128)} %bitcast.17, s32[]{:T(128)} %bitcast.16), kind=kLoop, calls=%fused_computation.36 | loop fusion | flops 11776 | bytes 2076 | tf_op jit(solution)/shard_map/gather | solution.py:97
  227.6 0.7 fusion.22
  228.3 0.6 add_minimum_fusion
  228.9 0.6 convert_compare_fusion
  229.6 4.4 %compare_select_fusion.4 = s32[512,1]{0,1:T(1,128)S(1)} fusion(s32[]{:T(128)} %bitcast.20, s32[]{:T(128)} %bitcast.21, s32[]{:T(128)} %bitcast.22, s32[]{:T(128)} %bitcast.23, s32[]{:T(128)} %bitcast.24, s32[]{:T(128)} %bitcast.26, s32[]{:T(128)} %bitcast.25, s32[512,1]{0,1:T(1,128)S(1)} %bitcast.49), kind=kLoop, calls=%fused_computation.29 | loop fusion | flops 7680 | bytes 4124 | tf_op jit(solution)/shard_map/gather | solution.py:99
  234.0 5.6 %fusion.8 = s32[512]{0:T(512)S(1)} fusion(pred[512]{0:T(512)(128)(4,1)S(1)} %get-tuple-element.13, pred[512]{0:T(512)(128)(4,1)S(1)} %get-tuple-element.12, pred[512]{0:T(512)(128)(4,1)S(1)} %compare_reduce_fusion.1, s32[512]{0:T(512)S(1)} %bitcast.50, s32[]{:T(128)} %bitcast.26, s32[]{:T(128)} %bitcast.19, s32[]{:T(128)} %bitcast.20, s32[]{:T(128)} %bitcast.21, ...), kind=kLoop, calls=%fused_computation.50 | loop fusion | flops 11776 | bytes 8228 | tf_op jit(solution)/shard_map/jit(_where)/select_n | solution.py:102
  239.6 1.0 fusion.1.rim_ref
  240.6 0.8 compare_select_fusion.1
  241.4 0.8 broadcast_multiply_fusion.inverse_ref
  242.3 94.0 %all-to-all-done.1.back_ref = f32[16,648,128]{2,1,0:T(8,128)} async-done(((f32[16,648,128]{2,1,0:T(8,128)}), f32[16,648,128]{2,1,0:T(8,128)}, u32[]{:S(2)}, u32[]{:S(2)}) %all-to-all-start.1) | async-done | bytes 5308448 | tf_op jit(solution)/shard_map/all_to_all | solution.py:652
  336.3 29.5 %sweeps.1 = f32[10,256,512]{2,1,0:T(8,128)} custom-call(f32[10,256,512]{2,1,0:T(8,128)} %bitcast.37, f32[16,648,128]{2,1,0:T(8,128)} %all-to-all-done.1.back_ref, f32[1,512]{1,0:T(1,128)} %bitcast.51, f32[25,512]{1,0:T(8,128)} %matrix_ref.1, f32[2,256,256]{2,1,0:T(8,128)} %broadcast_multiply_fusion.inverse_ref, bf16[512,512]{1,0:T(8,128)(2,1)} %fusion.1.rim_ref, ...), custom_call_target="tpu_custom_call" | custom-call | tf_op jit(solution)/shard_map/sweeps/pallas_call | solution.py:654
  365.8 8.9 %copy.28 = f32[2,5,256,512]{3,0,1,2:T(2,128)} copy(f32[2,5,256,512]{3,2,1,0:T(8,128)} %bitcast.38) | data formatting | bytes 10485760 | tf_op jit(solution)/shard_map/reshape | solution.py:663
  (10 shorter events, 0.1 us)
Async XLA Ops:
  15.8 6.7 %copy-start.3 = (s32[4096,2]{0,1:T(2,128)S(1)}, s32[4096,2]{0,1:T(2,128)}, u32[]{:S(2)}) copy-start(s32[4096,2]{0,1:T(2,128)} %param.12) | copy-start | bytes 98308
  15.8 121.6 %all-to-all-start = ((f32[16,640,128]{2,1,0:T(8,128)}), f32[16,640,128]{2,1,0:T(8,128)}, u32[]{:S(2)}, u32[]{:S(2)}) async-start(f32[16,640,128]{2,1,0:T(8,128)} %pack.1), calls=%async_computation | async-start | bytes 10485760 | tf_op jit(solution)/shard_map/all_to_all | solution.py:621
  22.5 158.8 %copy-start.4 = (f32[64,64]{1,0:T(8,128)S(1)}, f32[64,64]{1,0:T(8,128)}, u32[]{:S(2)}) copy-start(f32[64,64]{1,0:T(8,128)} %param.17) | copy-start | bytes 49156
  23.2 159.6 %copy-start.2 = (s32[4096,1]{0,1:T(1,128)S(1)}, s32[4096,1]{0,1:T(1,128)}, u32[]{:S(2)}) copy-start(s32[4096,1]{0,1:T(1,128)} %get-tuple-element.22) | copy-start | bytes 49156
  181.2 5.1 %collective-permute-start = (f32[40,128,128]{2,1,0:T(8,128)}, f32[40,128,128]{2,1,0:T(8,128)S(1)}, u32[]{:S(2)}, u32[]{:S(2)}) collective-permute-start(f32[40,128,128]{2,1,0:T(8,128)} %get-tuple-element.8.field_ref), channel_id=1, source_target_pairs={{0,1},{1,0},{2,3},{3,2},{4,5},{5,4},{6,7},{7,6},{8,9},{9,8},{10,11... | collective-permute-start | bytes 7864328 | tf_op jit(solution)/shard_map/ppermute | solution.py:634
  186.3 1.6 copy-start
  214.9 5.9 %copy-start.1 = (f32[8,64,64]{2,1,0:T(8,128)S(1)}, f32[8,64,64]{2,1,0:T(8,128)}, u32[]{:S(2)}) copy-start(f32[8,64,64]{2,1,0:T(8,128)} %param.16) | copy-start | bytes 393220
  214.9 6.8 %copy-start.5 = (s32[8]{0:T(128)S(1)}, s32[8]{0:T(128)}, u32[]{:S(2)}) copy-start(s32[8]{0:T(128)} %param.13) | copy-start | bytes 100
  214.9 121.4 %all-to-all-start.1 = ((f32[16,648,128]{2,1,0:T(8,128)}), f32[16,648,128]{2,1,0:T(8,128)}, u32[]{:S(2)}, u32[]{:S(2)}) async-start(f32[16,648,128]{2,1,0:T(8,128)} %force.1), calls=%async_computation.1 | async-start | bytes 10616832 | tf_op jit(solution)/shard_map/all_to_all | solution.py:652

commit v2 on v1

--- a/solution.py
+++ b/solution.py
@@ -1,3 +1,4 @@
+import functools
 import math
 
 import jax
@@ -287,7 +288,25 @@
     return jnp.where(which < 2, low, high)
 
 
-def pack_kernel(amp_ref, out_ref):
+def halves(first, second, wide):
+    return jnp.where(wide, first, shifted(second, 2))
+
+
+def pack_first_kernel(amp_ref, out_ref):
+    which = lane_group((8, LANES))
+
+    def body(step, carry):
+        rows = pl.ds(pl.multiple_of(step * 8, 8), 8)
+        for tile in range(4):
+            parts = [amp_ref[c, rows, tile * LANES : (tile + 1) * LANES] for c in (2, 3, 7, 8)]
+            for q in range(4):
+                out_ref[tile * 4 + q, rows, :] = join([shifted(parts[k], k - q) for k in range(4)], which)
+        return carry
+
+    lax.fori_loop(0, amp_ref.shape[1] // 8, body, 0)
+
+
+def pack_second_kernel(amp_ref, out_ref):
     half = amp_ref.shape[1] // 2
     full = 2 * half
     which = lane_group((8, LANES))
@@ -295,46 +314,43 @@
     def body(step, carry):
         row = pl.multiple_of(step * 8, 8)
         for tile in range(4):
-            lanes = pl.ds(tile * LANES, LANES)
-            rims = []
+            lanes = slice(tile * LANES, (tile + 1) * LANES)
+            rest = []
             for side in range(2):
                 rows = pl.ds(row + side * half, 8)
-                parts = [amp_ref[c, rows, lanes] for c in range(10)]
-                rims += [parts[4], parts[9]]
+                parts = [amp_ref[c, rows, lanes] for c in (0, 1, 5, 6)]
+                rest += [amp_ref[c, rows, lanes] for c in (4, 9)]
                 for q in range(4):
-                    dest = tile * 4 + q
-                    for block, first in ((0, 0), (1, 5)):
-                        out_ref[dest, pl.ds(row + side * half + block * full, 8), :] = join(
-                            [shifted(parts[first + k], k - q) for k in range(4)], which
-                        )
+                    out_ref[tile * 4 + q, rows, :] = join([shifted(parts[k], k - q) for k in range(4)], which)
             for q in range(4):
-                out_ref[tile * 4 + q, pl.ds(row + 2 * full, 8), :] = join(
-                    [shifted(rims[k], k - q) for k in range(4)], which
+                out_ref[tile * 4 + q, pl.ds(row + full, 8), :] = join(
+                    [shifted(rest[k], k - q) for k in range(4)], which
                 )
         return carry
 
     lax.fori_loop(0, half // 8, body, 0)
 
 
-def physical_kernel(pos_ref, in_ref, high_ref, low_ref, field_ref, span_ref, mean_ref, ga, gb, gc, mid):
+def physical_kernel(with_rest, pos_ref, in_ref, high_ref, low_ref, field_ref, span_ref, mean_ref, ga, gc, mid):
     sources = in_ref.shape[0]
-    half = M // sources // 2
-    full = 2 * half
+    full = M // sources
+    half = full // 2
 
     def spread(source, carry):
         def rows_of(step, inner):
             row = pl.multiple_of(step * 8, 8)
-            rest = in_ref[source, pl.ds(row + 2 * full, 8), :]
+            if with_rest:
+                rest = in_ref[source, pl.ds(row + full, 8), :]
             for side in range(2):
                 first = row + side * half
                 a8 = in_ref[source, pl.ds(first, 8), :]
-                b8 = in_ref[source, pl.ds(first + full, 8), :]
-                c8 = shifted(rest, 2 * side)
+                if with_rest:
+                    c8 = shifted(rest, 2 * side)
                 for u in range(8):
                     where = pos_ref[source * full + first + u]
                     ga[pl.ds(where, 1), :] = a8[u : u + 1, :]
-                    gb[pl.ds(where, 1), :] = b8[u : u + 1, :]
-                    gc[pl.ds(where, 1), :] = c8[u : u + 1, :]
+                    if with_rest:
+                        gc[pl.ds(where, 1), :] = c8[u : u + 1, :]
             return inner
 
         return lax.fori_loop(0, half // 8, rows_of, carry)
@@ -342,39 +358,50 @@
     lax.fori_loop(0, sources, spread, 0)
     mean_ref[...] = jnp.broadcast_to(ga[0:1, :], mean_ref.shape)
 
-    first_group = lane_group((NB, LANES)) == 0
-
-    def beta_sum(omega, carry):
-        rows = pl.ds(pl.multiple_of(omega * NB, NB), NB)
-        rest = gc[rows, :]
+    tall = lane_group((NB, LANES))
+
+    def store(omega, group, out, count):
+        for part in range(2):
+            mid[omega, (2 * group + part) * NB : (2 * group + part + 1) * NB, :] = jnp.where(
+                tall < count,
+                out[part * NB : (part + 1) * NB],
+                shifted(out[(2 + part) * NB : (3 + part) * NB], count),
+            )
+
+    def beta_sum(step, carry):
+        if with_rest:
+            rows = pl.ds(pl.multiple_of(step * NB, NB), NB)
+            first, second, turn = ga[rows, :], gc[rows, :], 3
+        else:
+            first = ga[pl.ds(pl.multiple_of(step * 2 * NB, NB), NB), :]
+            second, turn = ga[pl.ds(pl.multiple_of(step * 2 * NB + NB, NB), NB), :], 2
         data = jnp.concatenate(
             [
-                jnp.concatenate([ga[rows, :], rest], 1),
-                jnp.concatenate([gb[rows, :], shifted(rest, 3)], 1),
+                jnp.concatenate([first, second], 1),
+                jnp.concatenate([shifted(first, 2), shifted(second, turn)], 1),
             ],
             0,
         )
         out = dot3((high_ref[...], low_ref[...]), split(data))
-        mid[omega, 0 : 4 * NB, :] = out[:, :LANES]
-        tail = out[:, LANES:]
-        for part in range(2):
-            mid[omega, (4 + part) * NB : (5 + part) * NB, :] = jnp.where(
-                first_group,
-                tail[part * NB : (part + 1) * NB],
-                shifted(tail[(2 + part) * NB : (3 + part) * NB], 1),
-            )
-        return carry
-
-    lax.fori_loop(0, NW, beta_sum, 0)
+        if with_rest:
+            store(step, 0, out[:, :LANES], 2)
+            store(step, 1, out[:, LANES:], 1)
+        else:
+            store(2 * step, 0, out[:, :LANES], 2)
+            store(2 * step + 1, 0, out[:, LANES:], 2)
+        return carry
+
+    lax.fori_loop(0, NW if with_rest else NW // 2, beta_sum, 0)
 
     which = lane_group((8, LANES))
+    half_w = NW // 2
 
     def omega_sum(step, carry):
         row = pl.multiple_of(step * 8, 8)
-        for group in range(3):
+        rows = pl.ds(row, 8)
+        for group in range(2 if with_rest else 1):
             re = [mid[w, pl.ds(row + 2 * group * NB, 8), :] for w in range(NW)]
             im = [mid[w, pl.ds(row + (2 * group + 1) * NB, 8), :] for w in range(NW)]
-            half_w = NW // 2
             cos_terms = [re[0]] + [re[w] + re[NW - w] for w in range(1, half_w)] + [re[half_w]]
             sin_terms = [None] + [im[w] - im[NW - w] for w in range(1, half_w)]
             even = cosine_sums(cos_terms)
@@ -385,14 +412,14 @@
             for t in range(1, half_w):
                 out[t] = even[t] - odd[t]
                 out[NW - t] = even[t] + odd[t]
-            if group < 2:
-                target = (field_ref, span_ref)[group]
-                for t in range(NW):
-                    target[t, pl.ds(row, 8), :] = out[t]
+            if group == 0:
+                for t in range(half_w):
+                    field_ref[t, rows, :] = halves(out[t], out[t + half_w], which < 2)
+                    span_ref[t, rows, :] = jnp.where(which < 2, shifted(out[t], 2), out[t + half_w])
             else:
                 for t in range(8):
                     for target, start in ((field_ref, 0), (span_ref, 1)):
-                        target[NW + t, pl.ds(row, 8), :] = join(
+                        target[half_w + t, rows, :] = join(
                             [shifted(out[t + 8 * k], k - start) for k in range(4)], which
                         )
         return carry
@@ -401,46 +428,48 @@
 
 
 def force_kernel(
-    pos_ref, field_ref, other_ref, span_ref, mean_ref, wall_ref, high_ref, low_ref, out_ref,
-    force, mid, na, nb, nc, rest_rows,
+    with_rest, pos_ref, flow_ref, field_ref, other_ref, span_ref, mean_ref, wall_ref, high_ref, low_ref,
+    out_ref, force, mid, na, nc, rest_rows,
 ):
     sources = out_ref.shape[0]
-    half = M // sources // 2
-    full = 2 * half
+    full = M // sources
+    half = full // 2
     wall = split(wall_ref[...])
+    half_w = NW // 2
+    tall = lane_group((NB, LANES))
+    is_even = (tall % 2) == 0
 
     def products(step, carry):
-        which = lane_group((NB, LANES))
-
-        def gradient(row):
+        def one(row, v, w):
             both = jnp.concatenate([field_ref[row], other_ref[row]], 1)
-            return dot3(split(both), wall)
-
-        packed_v = packed_w = None
-        for k in range(4):
-            t = step + 8 * k
-            own = field_ref[t]
-            v = join([shifted(own, j - 2) for j in range(4)], which)
-            w = join([shifted(own, j - 3) for j in range(4)], which)
-            force[t] = -(v * gradient(t) + w * span_ref[t])
-            packed_v = v if k == 0 else jnp.where(which == k, v, packed_v)
-            packed_w = w if k == 0 else jnp.where(which == k, w, packed_w)
-        t = step + NW
-        force[t] = -(packed_v * gradient(t) + packed_w * span_ref[t])
+            force[row] = -(v * dot3(split(both), wall) + w * span_ref[row])
+
+        pair = [flow_ref[step], flow_ref[step + 8]]
+        for k in range(2):
+            one(
+                step + 8 * k,
+                jnp.where(is_even, pair[k], shifted(pair[k], 1)),
+                jnp.where(is_even, shifted(pair[k], 3), pair[k]),
+            )
+        if with_rest:
+            one(
+                step + half_w,
+                jnp.where(is_even, pair[0], shifted(pair[1], 1)),
+                jnp.where(is_even, shifted(pair[0], 3), pair[1]),
+            )
         return carry
 
     lax.fori_loop(0, 8, products, 0)
-
-    half_w = NW // 2
 
     def time_sum(step, carry):
         row = pl.multiple_of(step * 8, 8)
         rows = pl.ds(row, 8)
-        for group in range(2):
+        for group in range(2 if with_rest else 1):
             if group == 0:
-                values = [force[t, rows, :] for t in range(NW)]
+                packed = [force[t, rows, :] for t in range(half_w)]
+                values = packed + [shifted(value, 2) for value in packed]
             else:
-                packed = [force[NW + t, rows, :] for t in range(8)]
+                packed = [force[half_w + t, rows, :] for t in range(8)]
                 values = [shifted(packed[t % 8], -(t // 8)) for t in range(NW)]
             cos_terms = (
                 [values[0]]
@@ -459,19 +488,15 @@
 
     lax.fori_loop(0, NB // 8, time_sum, 0)
 
-    first_group = lane_group((NB, LANES)) == 0
-
     def span_sum(omega, carry):
         out = dot3((high_ref[...], low_ref[...]), split(mid[omega]))
         rows = pl.ds(pl.multiple_of(omega * NB, NB), NB)
-        na[rows, :] = out[:NB, :LANES]
-        nb[rows, :] = out[NB:, :LANES]
-        nc[rows, :] = jnp.where(first_group, out[:NB, LANES:], shifted(out[NB:, LANES:], 1))
+        na[rows, :] = halves(out[:NB, :LANES], out[NB:, :LANES], tall < 2)
+        if with_rest:
+            nc[rows, :] = jnp.where(tall < 1, out[:NB, LANES:], shifted(out[NB:, LANES:], 1))
         return carry
 
     lax.fori_loop(0, half_w + 1, span_sum, 0)
-
-    which = lane_group((8, LANES))
 
     def collect(source, carry):
         def rows_of(step, inner):
@@ -481,23 +506,24 @@
                 for u in range(8):
                     where = pos_ref[source * full + first + u]
                     out_ref[source, pl.ds(first + u, 1), :] = na[pl.ds(where, 1), :]
-                    out_ref[source, pl.ds(first + full + u, 1), :] = nb[pl.ds(where, 1), :]
-                    rest_rows[side, pl.ds(row + u, 1), :] = nc[pl.ds(where, 1), :]
+                    if with_rest:
+                        rest_rows[side, pl.ds(row + u, 1), :] = nc[pl.ds(where, 1), :]
             return inner
 
         lax.fori_loop(0, half // 8, rows_of, 0)
-        wide = lane_group((half, LANES)) < 2
-        out_ref[source, 2 * full : 2 * full + half, :] = jnp.where(
-            wide, rest_rows[0], shifted(rest_rows[1], 2)
-        )
-        out_ref[source, 2 * full + half : 2 * full + half + 8, :] = mean_ref[...]
+        if with_rest:
+            out_ref[source, full : full + half, :] = halves(
+                rest_rows[0], rest_rows[1], lane_group((half, LANES)) < 2
+            )
+        else:
+            out_ref[source, full : full + 8, :] = mean_ref[...]
         return carry
 
     lax.fori_loop(0, sources, collect, 0)
 
 
 def sweep_kernel(
-    amp_ref, back_ref, base_ref, matrix_ref, inverse_ref, rim_ref, wave_ref, freq_ref, sign_ref,
+    amp_ref, first_ref, second_ref, base_ref, matrix_ref, inverse_ref, rim_ref, wave_ref, freq_ref, sign_ref,
     out_ref, right, current, residual, flow,
 ):
     half = amp_ref.shape[1] // 2
@@ -506,10 +532,7 @@
     which = lane_group((rows_in, LANES))
     which8 = lane_group((8, LANES))
     for tile in range(4):
-        mean = join(
-            [shifted(back_ref[4 * tile + k, 2 * full + half : 2 * full + half + 8, :], k - 3) for k in range(4)],
-            which8,
-        )
+        mean = join([shifted(first_ref[4 * tile + k, full : full + 8, :], k - 1) for k in range(4)], which8)
         flow[:, tile * LANES : (tile + 1) * LANES] = mean + base_ref[:, tile * LANES : (tile + 1) * LANES]
     inverse = [split(inverse_ref[g]) for g in range(2)]
 
@@ -517,20 +540,20 @@
         row = pl.multiple_of(step * rows_in, rows_in)
         for tile in range(4):
             lanes = slice(tile * LANES, (tile + 1) * LANES)
-            rest = [back_ref[4 * tile + k, pl.ds(row + 2 * full, rows_in), :] for k in range(4)]
+            rest = [second_ref[4 * tile + k, pl.ds(row + full, rows_in), :] for k in range(4)]
             for side in range(2):
                 rows = pl.ds(row + side * half, rows_in)
                 sign = sign_ref[rows, :]
+                got = [
+                    [ref[4 * tile + k, rows, :] for k in range(4)] for ref in (second_ref, first_ref)
+                ]
                 for part in range(2):
-                    got = [
-                        back_ref[4 * tile + k, pl.ds(row + side * half + part * full, rows_in), :]
-                        for k in range(4)
-                    ]
                     for c in range(5):
                         if c < 4:
-                            value = join([shifted(got[k], k - c) for k in range(4)], which)
+                            source, place = got[c // 2], 2 * part + c % 2
                         else:
-                            value = join([shifted(rest[k], k - 2 * side - part) for k in range(4)], which)
+                            source, place = rest, 2 * side + part
+                        value = join([shifted(source[k], k - place) for k in range(4)], which)
                         if part == 1:
                             value = value * sign
                         own = amp_ref[5 * part + c, rows, lanes]
@@ -580,6 +603,10 @@
     params = pltpu.CompilerParams(vmem_limit_bytes=VMEM_BYTES)
     width = slab_inverse.shape[1]
 
+    def cost(micros):
+        return pl.CostEstimate(flops=micros * 10**9, bytes_accessed=micros * 3 * 10**6, transcendentals=0)
+
+
     omega_index = mode_table[:, 0]
     beta_index = mode_table[:, 1]
     grid_pos = omega_index * NB + beta_index
@@ -610,56 +637,88 @@
     rim = ((jnp.arange(points, dtype=jnp.int32)[:, None] == source[None, :]) & (weight[None, :] > 0)).astype(BF16)
 
     amp = jnp.transpose(amplitudes, (1, 2, 0, 3)).reshape(10, local_modes, points)
-    message = pl.pallas_call(
-        pack_kernel,
-        out_shape=jax.ShapeDtypeStruct((groups, 5 * half, LANES), F32),
-        in_specs=[vmem],
-        out_specs=vmem,
-        compiler_params=params,
-        name="pack",
-    )(amp)
-    arrived = lax.all_to_all(message, "modes", split_axis=0, concat_axis=0, tiled=True)
-
-    high, low = split_np(synthesis_matrix())
-    block = jax.ShapeDtypeStruct((NW + 8, NB, LANES), F32)
-    field, span, mean = pl.pallas_call(
-        physical_kernel,
-        out_shape=[block, block, jax.ShapeDtypeStruct((8, LANES), F32)],
-        in_specs=[smem, vmem, vmem, vmem],
-        out_specs=[vmem, vmem, vmem],
-        scratch_shapes=[pltpu.VMEM((M, LANES), F32)] * 3 + [pltpu.VMEM((NW, 6 * NB, LANES), F32)],
-        compiler_params=params,
-        name="physical",
-    )(grid_pos, arrived, jnp.asarray(high), jnp.asarray(low))
-    other = lax.ppermute(field, "modes", [(i, i ^ 1) for i in range(groups)])
-
-    high, low = split_np(analysis_matrix())
-    rows_back = (NW // 2 + 1) * NB
-    sendback = pl.pallas_call(
-        force_kernel,
-        out_shape=jax.ShapeDtypeStruct((groups, 5 * half + 8, LANES), F32),
-        in_specs=[smem] + [vmem] * 7,
-        out_specs=vmem,
-        scratch_shapes=[
-            pltpu.VMEM((NW + 8, NB, LANES), F32),
-            pltpu.VMEM((NW // 2 + 1, 2 * NB, 2 * LANES), F32),
-        ]
-        + [pltpu.VMEM((rows_back, LANES), F32)] * 3
-        + [pltpu.VMEM((2, half, LANES), F32)],
-        compiler_params=params,
-        name="force",
-    )(back_pos, field, other, span, mean, wall, jnp.asarray(high), jnp.asarray(low))
-    returned = lax.all_to_all(sendback, "modes", split_axis=0, concat_axis=0, tiled=True)
+    synthesis = [jnp.asarray(part) for part in split_np(synthesis_matrix())]
+    analysis = [jnp.asarray(part) for part in split_np(analysis_matrix())]
+    half_w = NW // 2
+    rows_back = (half_w + 1) * NB
+
+    def pack(kernel, source, rows, name):
+        return pl.pallas_call(
+            kernel,
+            out_shape=jax.ShapeDtypeStruct((groups, rows, LANES), F32),
+            in_specs=[vmem],
+            out_specs=vmem,
+            compiler_params=params,
+            cost_estimate=cost(6),
+            name=name,
+        )(source)
+
+    def exchange(message):
+        return lax.all_to_all(message, "modes", split_axis=0, concat_axis=0, tiled=True)
+
+    def physical(arrived, with_rest):
+        count = half_w + (8 if with_rest else 0)
+        block = jax.ShapeDtypeStruct((count, NB, LANES), F32)
+        kinds = 2 if with_rest else 1
+        return pl.pallas_call(
+            functools.partial(physical_kernel, with_rest),
+            out_shape=[block, block, jax.ShapeDtypeStruct((8, LANES), F32)],
+            in_specs=[smem, vmem, vmem, vmem],
+            out_specs=[vmem, vmem, vmem],
+            scratch_shapes=[
+                pltpu.VMEM((M, LANES), F32),
+                pltpu.VMEM((M if with_rest else 8, LANES), F32),
+                pltpu.VMEM((NW, 2 * kinds * NB, LANES), F32),
+            ],
+            compiler_params=params,
+            cost_estimate=cost(15 * kinds),
+            name="physical" + str(kinds),
+        )(grid_pos, arrived, *synthesis)
+
+    def swap(field):
+        return lax.ppermute(field, "modes", [(i, i ^ 1) for i in range(groups)])
+
+    def forces(flow, field, other, span, mean, with_rest):
+        kinds = 2 if with_rest else 1
+        return pl.pallas_call(
+            functools.partial(force_kernel, with_rest),
+            out_shape=jax.ShapeDtypeStruct((groups, 3 * half if with_rest else 2 * half + 8, LANES), F32),
+            in_specs=[smem] + [vmem] * 8,
+            out_specs=vmem,
+            scratch_shapes=[
+                pltpu.VMEM((half_w + 8, NB, LANES), F32),
+                pltpu.VMEM((half_w + 1, 2 * NB, kinds * LANES), F32),
+                pltpu.VMEM((rows_back, LANES), F32),
+                pltpu.VMEM((rows_back if with_rest else 8, LANES), F32),
+                pltpu.VMEM((2, half, LANES), F32),
+            ],
+            compiler_params=params,
+            cost_estimate=cost(10 * kinds),
+            name="force" + str(kinds),
+        )(back_pos, flow, field, other, span, mean, wall, *analysis)
+
+    first_message = pack(pack_first_kernel, amp, 2 * half, "pack1")
+    first_message, later = lax.optimization_barrier((first_message, amp))
+    first = exchange(first_message)
+    second_message = pack(pack_second_kernel, later, 3 * half, "pack2")
+    second = exchange(second_message)
+    first, second_message = lax.optimization_barrier((first, second_message))
+    flow, flow_span, mean = physical(first, False)
+    first_force = forces(flow, flow, swap(flow), flow_span, mean, False)
+    first_force, second = lax.optimization_barrier((first_force, second))
+    first_back = exchange(first_force)
+    field, span, unused = physical(second, True)
+    second_back = exchange(forces(flow, field, swap(field), span, unused, True))
 
     marched = pl.pallas_call(
         sweep_kernel,
         out_shape=jax.ShapeDtypeStruct((10, local_modes, points), F32),
-        in_specs=[vmem] * 9,
+        in_specs=[vmem] * 10,
         out_specs=vmem,
         scratch_shapes=[pltpu.VMEM((320, points), F32)] * 3 + [pltpu.VMEM((8, points), F32)],
         compiler_params=params,
         name="sweeps",
-    )(amp, returned, base_flow[None, :], base_coupling, inverse, rim, wave_local, freq_local, sign_local)
+    )(amp, first_back, second_back, base_flow[None, :], base_coupling, inverse, rim, wave_local, freq_local, sign_local)
     return jnp.transpose(marched.reshape(2, 5, local_modes, points), (2, 0, 1, 3))
 
 

time: 375 us -> 340 us (0.907)
  waiting for transfers between devices: 211 us -> 106 us
  Pallas kernels: 110 us -> 148 us
  local copies, waits for them, and re-layouts: 20.8 us -> 36.3 us
  starting transfers between devices: 11.9 us -> 23.1 us
  other arithmetic: 20.4 us -> 24.3 us
    all_to_all x2 -> x4, waiting for transfers between devices: 208 us -> 103 us  [exchange(): lax.all_to_all(message, 'modes', split_axis=0, concat_axis=0, tiled=True)]
    pallas_call x3 -> x6, Pallas kernels: 80.7 us -> 119 us  [the longest x2 62 us: physical(): pl.pallas_call(functools.partial(physical_kernel, with_rest), out_shape=[...]
    all_to_all x2 -> x4, starting transfers between devices: 11.7 us -> 22.4 us  [exchange(): lax.all_to_all(message, 'modes', split_axis=0, concat_axis=0, tiled=True)]
    mul x5, local copies, waits for them, and re-layouts: 1.4 us -> 8.86 us  [local_fast(): turned * eye[None, :, None, :, None]]
    unnamed x14 -> x27, local copies, waits for them, and re-layouts: 1.85 us -> 8.26 us
  transfers between devices with their start and end apart: 3 -> 6, of which waited for: 3 -> 4; matrix products, arithmetic and copies ran while one was open for 7% -> 11% of each run, Pallas kernels for 0% -> 33%
where the time goes in v2:
time: 340 us; the launch traced here: 339 us
  Pallas kernels  148 us (44%)
  waiting for transfers between devices  106 us (31%)
  local copies, waits for them, and re-layouts  36.3 us (11%)
  other arithmetic  24.3 us (7%)
  starting transfers between devices  23.1 us (7%)
    all_to_all x4, waiting for transfers between devices, exchange(): lax.all_to_all(message, 'modes', split_axis=0, concat_axis=0, tiled=True)  103 us
    pallas_call x2, Pallas kernels, physical(): pl.pallas_call(functools.partial(physical_kernel, with_rest), out_shape=[...  62 us
    pallas_call x2, Pallas kernels, forces(): pl.pallas_call(functools.partial(force_kernel, with_rest), out_shape=jax....  41.2 us
    pallas_call x1, Pallas kernels, local_fast(): pl.pallas_call(sweep_kernel, out_shape=jax.ShapeDtypeStruct((10, local_mo...  29.7 us
    all_to_all x4, starting transfers between devices, exchange(): lax.all_to_all(message, 'modes', split_axis=0, concat_axis=0, tiled=True)  22.4 us
    pallas_call x2, Pallas kernels, pack(): pl.pallas_call(kernel, out_shape=jax.ShapeDtypeStruct((groups, rows, LANE...  15.3 us
    reshape x1, local copies, waits for them, and re-layouts, local_fast(): marched.reshape(2, 5, local_modes, points)  8.89 us
    mul x5, local copies, waits for them, and re-layouts, local_fast(): turned * eye[None, :, None, :, None]  8.86 us
  transfers between devices with their start and end apart: 6, of which 4 were waited for; matrix products, arithmetic and copies ran while one was open for 11% of the time, Pallas kernels for 33%

profile of v2, /device:TPU:15, one launch (start us, length us, event | category | flops | bytes accessed | tf_op | source)
XLA Modules:
  0.0 338.6 jit_solution(9400258908511365281)
XLA Ops:
  0.0 5.9 %copy.18 = f32[2,5,256,512]{3,2,1,0:T(8,128)} copy(f32[2,5,256,512]{3,0,1,2:T(2,128)} %bitcast.40) | data formatting | bytes 10485760 | tf_op jit(solution)/shard_map/transpose | solution.py:639
  5.9 7.7 %pack1.1 = f32[16,256,128]{2,1,0:T(8,128)} custom-call(f32[10,256,512]{2,1,0:T(8,128)} %bitcast.36), custom_call_target="tpu_custom_call" | custom-call | flops 6000000000 | bytes 18000000 | tf_op jit(solution)/shard_map/pack1/pallas_call | solution.py:646
  13.5 6.6 %all-to-all-start = ((f32[16,256,128]{2,1,0:T(8,128)}), f32[16,256,128]{2,1,0:T(8,128)S(1)}, u32[]{:S(2)}, u32[]{:S(2)}) async-start(f32[16,256,128]{2,1,0:T(8,128)} %pack1.1), calls=%async_computation | async-start | bytes 4194304 | tf_op jit(solution)/shard_map/all_to_all | solution.py:657
  20.1 7.7 %pack2.1 = f32[16,384,128]{2,1,0:T(8,128)} custom-call(f32[10,256,512]{2,1,0:T(8,128)} %bitcast.37), custom_call_target="tpu_custom_call" | custom-call | flops 6000000000 | bytes 18000000 | tf_op jit(solution)/shard_map/pack2/pallas_call | solution.py:646
  27.7 39.8 %all-to-all-done.in_ref = f32[16,256,128]{2,1,0:T(8,128)S(1)} async-done(((f32[16,256,128]{2,1,0:T(8,128)}), f32[16,256,128]{2,1,0:T(8,128)S(1)}, u32[]{:S(2)}, u32[]{:S(2)}) %all-to-all-start) | async-done | bytes 2097184 | tf_op jit(solution)/shard_map/all_to_all | solution.py:657
  67.5 1.4 copy-done.3
  68.8 4.9 %all-to-all-start.1 = ((f32[16,384,128]{2,1,0:T(8,128)}), f32[16,384,128]{2,1,0:T(8,128)S(1)}, u32[]{:S(2)}, u32[]{:S(2)}) async-start(f32[16,384,128]{2,1,0:T(8,128)} %pack2.1), calls=%async_computation.1 | async-start | bytes 6291456 | tf_op jit(solution)/shard_map/all_to_all | solution.py:657
  73.8 0.7 slice_subtract_fusion
  74.4 19.1 %physical1.1 = (f32[16,128,128]{2,1,0:T(8,128)}, f32[16,128,128]{2,1,0:T(8,128)}, f32[8,128]{1,0:T(8,128)}) custom-call(s32[4096]{0:T(1024)} %bitcast.42, f32[16,256,128]{2,1,0:T(8,128)} %copy-done.3, bf16[512,256]{1,0:T(8,128)(2,1)} %constant.123.clone.high_ref, bf16[512,256]{1,0:T(8,128)(2,1)} %constant.124.clone.low_ref), custom_call_target="tpu_custom_call" | custom-call | flops 15000000512 | bytes 45000000 | tf_op jit(solution)/shard_map/physical1/pallas_call | solution.py:663
  93.5 0.4 collective-permute-start
  94.1 0.8 broadcast_multiply_fusion.1
  95.0 1.1 mul.101
  96.1 0.2 mul.104
  96.3 0.8 compare_reduce_fusion
  97.1 1.3 fusion.6.pos_ref
  98.5 18.2 %force1.1 = f32[16,264,128]{2,1,0:T(8,128)} custom-call(s32[4096]{0:T(1024)} %fusion.6.pos_ref, f32[16,128,128]{2,1,0:T(8,128)} %get-tuple-element.19.flow_ref.field_ref, f32[16,128,128]{2,1,0:T(8,128)} %get-tuple-element.19.flow_ref.field_ref, f32[16,128,128]{2,1,0:T(8,128)} %collective-permute-done.other_ref, f32[16,128,128]{2,1,0:T(8,128)} %get-tuple-element.20.span_ref, ...), custom_call_target="tpu_custom_call" | custom-call | flops 10000000000 | bytes 30000000 | tf_op jit(solution)/shard_map/force1/pallas_call | solution.py:683
  116.7 26.9 %all-to-all-done.1.in_ref = f32[16,384,128]{2,1,0:T(8,128)S(1)} async-done(((f32[16,384,128]{2,1,0:T(8,128)}), f32[16,384,128]{2,1,0:T(8,128)S(1)}, u32[]{:S(2)}, u32[]{:S(2)}) %all-to-all-start.1) | async-done | bytes 3145760 | tf_op jit(solution)/shard_map/all_to_all | solution.py:657
  143.6 1.6 copy-done.2
  145.3 4.9 %all-to-all-start.2 = ((f32[16,264,128]{2,1,0:T(8,128)}), f32[16,264,128]{2,1,0:T(8,128)S(1)}, u32[]{:S(2)}, u32[]{:S(2)}) async-start(f32[16,264,128]{2,1,0:T(8,128)} %force1.1), calls=%async_computation.2 | async-start | bytes 4325376 | tf_op jit(solution)/shard_map/all_to_all | solution.py:657
  150.2 42.9 %physical2.1 = (f32[24,128,128]{2,1,0:T(8,128)}, f32[24,128,128]{2,1,0:T(8,128)}, f32[8,128]{1,0:T(8,128)}) custom-call(s32[4096]{0:T(1024)} %bitcast.43, f32[16,384,128]{2,1,0:T(8,128)} %copy-done.2, bf16[512,256]{1,0:T(8,128)(2,1)} %constant.123.clone.high_ref, bf16[512,256]{1,0:T(8,128)(2,1)} %constant.124.clone.low_ref), custom_call_target="tpu_custom_call" | custom-call | flops 30000001024 | bytes 90000000 | tf_op jit(solution)/shard_map/physical2/pallas_call | solution.py:663
  193.1 0.4 collective-permute-start.1
  193.5 3.3 collective-permute-done.1.other_ref
  196.7 1.2 copy-done.11
  197.9 23.0 %force2.1 = f32[16,384,128]{2,1,0:T(8,128)} custom-call(s32[4096]{0:T(1024)} %fusion.6.pos_ref, f32[16,128,128]{2,1,0:T(8,128)} %get-tuple-element.19.flow_ref.field_ref, f32[24,128,128]{2,1,0:T(8,128)} %get-tuple-element.24.field_ref, f32[24,128,128]{2,1,0:T(8,128)} %copy-done.11, f32[24,128,128]{2,1,0:T(8,128)} %get-tuple-element.25.span_ref, ...), custom_call_target="tpu_custom_call" | custom-call | flops 20000000000 | bytes 60000000 | tf_op jit(solution)/shard_map/force2/pallas_call | solution.py:683
  220.9 1.4 copy-done.1
  222.4 6.0 %all-to-all-start.3 = ((f32[16,384,128]{2,1,0:T(8,128)}), f32[16,384,128]{2,1,0:T(8,128)S(1)}, u32[]{:S(2)}, u32[]{:S(2)}) async-start(f32[16,384,128]{2,1,0:T(8,128)} %force2.1), calls=%async_computation.3 | async-start | bytes 6291456 | tf_op jit(solution)/shard_map/all_to_all | solution.py:657
  228.4 0.8 constant_dynamic-slice_fusion
  229.4 0.8 copy.26
  230.2 0.9 mul.108
  231.1 1.4 mul.109
  232.5 1.8 copy.21
  234.3 2.1 mul.106
  236.4 2.6 mul.107
  239.0 0.8 scatter_custom_fusion
  239.9 0.7 fusion.23
  240.5 4.4 %compare_select_fusion.10 = s32[512,1]{0,1:T(1,128)S(1)} fusion(s32[]{:T(128)} %bitcast.11, s32[]{:T(128)} %bitcast.12, s32[]{:T(128)} %bitcast.13, s32[]{:T(128)} %bitcast.14, s32[]{:T(128)} %bitcast.15, s32[]{:T(128)} %bitcast.17, s32[]{:T(128)} %bitcast.16), kind=kLoop, calls=%fused_computation.35 | loop fusion | flops 11776 | bytes 2076 | tf_op jit(solution)/shard_map/gather | solution.py:98
  245.0 0.7 fusion.22
  245.6 0.7 add_minimum_fusion
  246.4 0.7 convert_compare_fusion
  247.0 4.4 %compare_select_fusion.4 = s32[512,1]{0,1:T(1,128)S(1)} fusion(s32[]{:T(128)} %bitcast.20, s32[]{:T(128)} %bitcast.21, s32[]{:T(128)} %bitcast.22, s32[]{:T(128)} %bitcast.23, s32[]{:T(128)} %bitcast.24, s32[]{:T(128)} %bitcast.26, s32[]{:T(128)} %bitcast.25, s32[512,1]{0,1:T(1,128)S(1)} %bitcast.51), kind=kLoop, calls=%fused_computation.28 | loop fusion | flops 7680 | bytes 4124 | tf_op jit(solution)/shard_map/gather | solution.py:100
  251.5 5.7 %fusion.8 = s32[512]{0:T(512)S(1)} fusion(pred[512]{0:T(512)(128)(4,1)S(1)} %get-tuple-element.29, pred[512]{0:T(512)(128)(4,1)S(1)} %get-tuple-element.28, pred[512]{0:T(512)(128)(4,1)S(1)} %compare_reduce_fusion.1, s32[512]{0:T(512)S(1)} %bitcast.52, s32[]{:T(128)} %bitcast.26, s32[]{:T(128)} %bitcast.19, s32[]{:T(128)} %bitcast.20, s32[]{:T(128)} %bitcast.21, ...), kind=kLoop, calls=%fused_computation.51 | loop fusion | flops 11776 | bytes 8228 | tf_op jit(solution)/shard_map/jit(_where)/select_n | solution.py:103
  257.2 1.0 fusion.1.rim_ref
  258.2 1.7 compare_select_fusion.1
  260.0 1.9 broadcast_multiply_fusion.inverse_ref
  261.9 36.4 %all-to-all-done.3.second_ref = f32[16,384,128]{2,1,0:T(8,128)S(1)} async-done(((f32[16,384,128]{2,1,0:T(8,128)}), f32[16,384,128]{2,1,0:T(8,128)S(1)}, u32[]{:S(2)}, u32[]{:S(2)}) %all-to-all-start.3) | async-done | bytes 3145760 | tf_op jit(solution)/shard_map/all_to_all | solution.py:657
  298.3 1.7 copy-done
  300.0 29.7 %sweeps.1 = f32[10,256,512]{2,1,0:T(8,128)} custom-call(f32[10,256,512]{2,1,0:T(8,128)} %bitcast.38, f32[16,264,128]{2,1,0:T(8,128)} %copy-done.1, f32[16,384,128]{2,1,0:T(8,128)} %copy-done, f32[1,512]{1,0:T(1,128)} %bitcast.53, f32[25,512]{1,0:T(8,128)} %matrix_ref.1, f32[2,256,256]{2,1,0:T(8,128)} %broadcast_multiply_fusion.inverse_ref, ...), custom_call_target="tpu_custom_call" | custom-call | tf_op jit(solution)/shard_map/sweeps/pallas_call | solution.py:713
  329.7 8.9 %copy.28 = f32[2,5,256,512]{3,0,1,2:T(2,128)} copy(f32[2,5,256,512]{3,2,1,0:T(8,128)} %bitcast.39) | data formatting | bytes 10485760 | tf_op jit(solution)/shard_map/reshape | solution.py:722
  (32 shorter events, 0.5 us)
Async XLA Ops:
  13.5 54.0 %all-to-all-start = ((f32[16,256,128]{2,1,0:T(8,128)}), f32[16,256,128]{2,1,0:T(8,128)S(1)}, u32[]{:S(2)}, u32[]{:S(2)}) async-start(f32[16,256,128]{2,1,0:T(8,128)} %pack1.1), calls=%async_computation | async-start | bytes 4194304 | tf_op jit(solution)/shard_map/all_to_all | solution.py:657
  27.7 46.0 %copy-start.4 = (s32[4096,2]{0,1:T(2,128)S(1)}, s32[4096,2]{0,1:T(2,128)}, u32[]{:S(2)}) copy-start(s32[4096,2]{0,1:T(2,128)} %param.12) | copy-start | bytes 98308
  67.5 1.4 copy-start.3
  68.8 74.8 %all-to-all-start.1 = ((f32[16,384,128]{2,1,0:T(8,128)}), f32[16,384,128]{2,1,0:T(8,128)S(1)}, u32[]{:S(2)}, u32[]{:S(2)}) async-start(f32[16,384,128]{2,1,0:T(8,128)} %pack2.1), calls=%async_computation.1 | async-start | bytes 6291456 | tf_op jit(solution)/shard_map/all_to_all | solution.py:657
  74.4 19.5 %copy-start.7 = (f32[64,64]{1,0:T(8,128)S(1)}, f32[64,64]{1,0:T(8,128)}, u32[]{:S(2)}) copy-start(f32[64,64]{1,0:T(8,128)} %param.17) | copy-start | bytes 49156
  74.4 22.7 %copy-start.5 = (s32[4096,1]{0,1:T(1,128)S(1)}, s32[4096,1]{0,1:T(1,128)}, u32[]{:S(2)}) copy-start(s32[4096,1]{0,1:T(1,128)} %get-tuple-element.38) | copy-start | bytes 49156
  93.5 5.0 %collective-permute-start = (f32[16,128,128]{2,1,0:T(8,128)}, f32[16,128,128]{2,1,0:T(8,128)}, u32[]{:S(2)}, u32[]{:S(2)}) collective-permute-start(f32[16,128,128]{2,1,0:T(8,128)} %get-tuple-element.19.flow_ref.field_ref), channel_id=1, source_target_pairs={{0,1},{1,0},{2,3},{3,2},{4,5},{5,4},{6,7},{7,6},{8,9},{9,8},{10,11... | collective-permute-start | bytes 3145736 | tf_op jit(solution)/shard_map/ppermute | solution.py:679
  94.1 0.8 copy-start.9
  96.3 2.2 copy-start.6
  143.6 1.6 copy-start.2
  145.3 75.6 %all-to-all-start.2 = ((f32[16,264,128]{2,1,0:T(8,128)}), f32[16,264,128]{2,1,0:T(8,128)S(1)}, u32[]{:S(2)}, u32[]{:S(2)}) async-start(f32[16,264,128]{2,1,0:T(8,128)} %force1.1), calls=%async_computation.2 | async-start | bytes 4325376 | tf_op jit(solution)/shard_map/all_to_all | solution.py:657
  193.1 3.6 %collective-permute-start.1 = (f32[24,128,128]{2,1,0:T(8,128)}, f32[24,128,128]{2,1,0:T(8,128)S(1)}, u32[]{:S(2)}, u32[]{:S(2)}) collective-permute-start(f32[24,128,128]{2,1,0:T(8,128)} %get-tuple-element.24.field_ref), channel_id=1, source_target_pairs={{0,1},{1,0},{2,3},{3,2},{4,5},{5,4},{6,7},{7,6},{8,9},{9,8},{10,11... | collective-permute-start | bytes 4718600 | tf_op jit(solution)/shard_map/ppermute | solution.py:679
  196.7 1.2 copy-start.11
  220.9 9.2 %copy-start.10 = (f32[4,4]{1,0:T(4,128)S(1)}, f32[4,4]{1,0:T(4,128)}, u32[]{:S(2)}) copy-start(f32[4,4]{1,0:T(4,128)} %copy-done.9) | copy-start | bytes 196
  220.9 1.4 copy-start.1
  222.4 75.9 %all-to-all-start.3 = ((f32[16,384,128]{2,1,0:T(8,128)}), f32[16,384,128]{2,1,0:T(8,128)S(1)}, u32[]{:S(2)}, u32[]{:S(2)}) async-start(f32[16,384,128]{2,1,0:T(8,128)} %force2.1), calls=%async_computation.3 | async-start | bytes 6291456 | tf_op jit(solution)/shard_map/all_to_all | solution.py:657
  228.4 10.6 %copy-start.8 = (s32[8]{0:T(128)S(1)}, s32[8]{0:T(128)}, u32[]{:S(2)}) copy-start(s32[8]{0:T(128)} %param.13) | copy-start | bytes 100
  298.3 1.7 copy-start

commit v3 on v2

--- a/solution.py
+++ b/solution.py
@@ -292,34 +292,38 @@
     return jnp.where(wide, first, shifted(second, 2))
 
 
+def channel(amp_ref, c, row, count, tile):
+    return amp_ref[pl.ds(row * 40 + (c % 5) * 8 + tile * 2 + c // 5, count, stride=40), :]
+
+
 def pack_first_kernel(amp_ref, out_ref):
     which = lane_group((8, LANES))
 
     def body(step, carry):
-        rows = pl.ds(pl.multiple_of(step * 8, 8), 8)
+        row = pl.multiple_of(step * 8, 8)
+        rows = pl.ds(row, 8)
         for tile in range(4):
-            parts = [amp_ref[c, rows, tile * LANES : (tile + 1) * LANES] for c in (2, 3, 7, 8)]
+            parts = [channel(amp_ref, c, row, 8, tile) for c in (2, 3, 7, 8)]
             for q in range(4):
                 out_ref[tile * 4 + q, rows, :] = join([shifted(parts[k], k - q) for k in range(4)], which)
         return carry
 
-    lax.fori_loop(0, amp_ref.shape[1] // 8, body, 0)
+    lax.fori_loop(0, amp_ref.shape[0] // 320, body, 0)
 
 
 def pack_second_kernel(amp_ref, out_ref):
-    half = amp_ref.shape[1] // 2
+    half = amp_ref.shape[0] // 80
     full = 2 * half
     which = lane_group((8, LANES))
 
     def body(step, carry):
         row = pl.multiple_of(step * 8, 8)
         for tile in range(4):
-            lanes = slice(tile * LANES, (tile + 1) * LANES)
             rest = []
             for side in range(2):
                 rows = pl.ds(row + side * half, 8)
-                parts = [amp_ref[c, rows, lanes] for c in (0, 1, 5, 6)]
-                rest += [amp_ref[c, rows, lanes] for c in (4, 9)]
+                parts = [channel(amp_ref, c, row + side * half, 8, tile) for c in (0, 1, 5, 6)]
+                rest += [channel(amp_ref, c, row + side * half, 8, tile) for c in (4, 9)]
                 for q in range(4):
                     out_ref[tile * 4 + q, rows, :] = join([shifted(parts[k], k - q) for k in range(4)], which)
             for q in range(4):
@@ -526,7 +530,7 @@
     amp_ref, first_ref, second_ref, base_ref, matrix_ref, inverse_ref, rim_ref, wave_ref, freq_ref, sign_ref,
     out_ref, right, current, residual, flow,
 ):
-    half = amp_ref.shape[1] // 2
+    half = amp_ref.shape[0] // 80
     full = 2 * half
     rows_in = 16
     which = lane_group((rows_in, LANES))
@@ -556,7 +560,7 @@
                         value = join([shifted(source[k], k - place) for k in range(4)], which)
                         if part == 1:
                             value = value * sign
-                        own = amp_ref[5 * part + c, rows, lanes]
+                        own = channel(amp_ref, 5 * part + c, row + side * half, rows_in, tile)
                         place = slice((5 * part + c) * 32 + side * 16, (5 * part + c) * 32 + side * 16 + 16)
                         current[place, lanes] = own
                         right[place, lanes] = own + march_step * value
@@ -584,9 +588,11 @@
                 current[:, lanes] = dot3(split(residual[:, lanes]), inverse[g])
         for c in range(10):
             for side in range(2):
-                out_ref[c, pl.ds(row + side * half, rows_in), :] = current[
-                    c * 32 + side * 16 : c * 32 + side * 16 + 16, :
-                ]
+                for tile in range(4):
+                    offset = (row + side * half) * 40 + (c % 5) * 8 + tile * 2 + c // 5
+                    out_ref[pl.ds(offset, rows_in, stride=40), :] = current[
+                        c * 32 + side * 16 : c * 32 + side * 16 + 16, tile * LANES : (tile + 1) * LANES
+                    ]
         return carry
 
     lax.fori_loop(0, half // rows_in, chunk, 0)
@@ -636,7 +642,8 @@
     source, weight = interface_table(slab_map, slab_inverse.shape[0], width)
     rim = ((jnp.arange(points, dtype=jnp.int32)[:, None] == source[None, :]) & (weight[None, :] > 0)).astype(BF16)
 
-    amp = jnp.transpose(amplitudes, (1, 2, 0, 3)).reshape(10, local_modes, points)
+    tiled = amplitudes.reshape(local_modes, 2, 5, points // LANES, LANES)
+    amp = jnp.transpose(tiled, (0, 2, 3, 1, 4)).reshape(local_modes * 40, LANES)
     synthesis = [jnp.asarray(part) for part in split_np(synthesis_matrix())]
     analysis = [jnp.asarray(part) for part in split_np(analysis_matrix())]
     half_w = NW // 2
@@ -712,14 +719,15 @@
 
     marched = pl.pallas_call(
         sweep_kernel,
-        out_shape=jax.ShapeDtypeStruct((10, local_modes, points), F32),
+        out_shape=jax.ShapeDtypeStruct((local_modes * 40, LANES), F32),
         in_specs=[vmem] * 10,
         out_specs=vmem,
         scratch_shapes=[pltpu.VMEM((320, points), F32)] * 3 + [pltpu.VMEM((8, points), F32)],
         compiler_params=params,
         name="sweeps",
     )(amp, first_back, second_back, base_flow[None, :], base_coupling, inverse, rim, wave_local, freq_local, sign_local)
-    return jnp.transpose(marched.reshape(2, 5, local_modes, points), (2, 0, 1, 3))
+    ordered = marched.reshape(local_modes, 5, points // LANES, 2, LANES)
+    return jnp.transpose(ordered, (0, 3, 1, 2, 4)).reshape(local_modes, 2, 5, points)
 
 
 def run(amplitudes, mode_table, slab_map, base_flow, base_coupling, slab_inverse, wall_operator):

time: 340 us -> 325 us (0.956)
  local copies, waits for them, and re-layouts: 36.3 us -> 21.3 us
    reshape x1 -> x0, local copies, waits for them, and re-layouts: 8.89 us -> none  [local_fast(): marched.reshape(2, 5, local_modes, points)]
    transpose x1 -> x0, local copies, waits for them, and re-layouts: 5.85 us -> none  [local_fast(): jnp.transpose(amplitudes, (1, 2, 0, 3)).reshape(10, local_modes, points)]
  transfers between devices with their start and end apart: 6 -> 6, of which waited for: 4 -> 4; matrix products, arithmetic and copies ran while one was open for 11% -> 12% of each run, Pallas kernels for 33% -> 34%
where the time goes in v3:
time: 325 us; the launch traced here: 324 us
  Pallas kernels  148 us (46%)
  waiting for transfers between devices  107 us (33%)
  other arithmetic  23.8 us (7%)
  starting transfers between devices  23.1 us (7%)
  local copies, waits for them, and re-layouts  21.3 us (7%)
    all_to_all x4, waiting for transfers between devices, exchange(): lax.all_to_all(message, 'modes', split_axis=0, concat_axis=0, tiled=True)  104 us
    pallas_call x2, Pallas kernels, physical(): pl.pallas_call(functools.partial(physical_kernel, with_rest), out_shape=[...  62 us
    pallas_call x2, Pallas kernels, forces(): pl.pallas_call(functools.partial(force_kernel, with_rest), out_shape=jax....  41.2 us
    pallas_call x1, Pallas kernels, local_fast(): pl.pallas_call(sweep_kernel, out_shape=jax.ShapeDtypeStruct((local_modes...  29.6 us
    all_to_all x4, starting transfers between devices, exchange(): lax.all_to_all(message, 'modes', split_axis=0, concat_axis=0, tiled=True)  22.4 us
    pallas_call x2, Pallas kernels, pack(): pl.pallas_call(kernel, out_shape=jax.ShapeDtypeStruct((groups, rows, LANE...  15.4 us
    mul x5, local copies, waits for them, and re-layouts, local_fast(): turned * eye[None, :, None, :, None]  8.87 us
    unnamed x27, local copies, waits for them, and re-layouts  8.2 us
  transfers between devices with their start and end apart: 6, of which 4 were waited for; matrix products, arithmetic and copies ran while one was open for 12% of the time, Pallas kernels for 34%

profile of v3, /device:TPU:15, one launch (start us, length us, event | category | flops | bytes accessed | tf_op | source)
XLA Modules:
  0.0 323.7 jit_solution(6945464440484137996)
XLA Ops:
  0.0 7.7 %pack1.1 = f32[16,256,128]{2,1,0:T(8,128)} custom-call(f32[10240,128]{1,0:T(8,128)} %bitcast.40), custom_call_target="tpu_custom_call" | custom-call | flops 6000000000 | bytes 18000000 | tf_op jit(solution)/shard_map/pack1/pallas_call | solution.py:653
  7.7 6.6 %all-to-all-start = ((f32[16,256,128]{2,1,0:T(8,128)}), f32[16,256,128]{2,1,0:T(8,128)S(1)}, u32[]{:S(2)}, u32[]{:S(2)}) async-start(f32[16,256,128]{2,1,0:T(8,128)} %pack1.1), calls=%async_computation | async-start | bytes 4194304 | tf_op jit(solution)/shard_map/all_to_all | solution.py:664
  14.2 7.7 %pack2.1 = f32[16,384,128]{2,1,0:T(8,128)} custom-call(f32[10240,128]{1,0:T(8,128)} %bitcast.41), custom_call_target="tpu_custom_call" | custom-call | flops 6000000000 | bytes 18000000 | tf_op jit(solution)/shard_map/pack2/pallas_call | solution.py:653
  21.9 39.7 %all-to-all-done.in_ref = f32[16,256,128]{2,1,0:T(8,128)S(1)} async-done(((f32[16,256,128]{2,1,0:T(8,128)}), f32[16,256,128]{2,1,0:T(8,128)S(1)}, u32[]{:S(2)}, u32[]{:S(2)}) %all-to-all-start) | async-done | bytes 2097184 | tf_op jit(solution)/shard_map/all_to_all | solution.py:664
  61.6 1.3 copy-done.3
  63.0 4.9 %all-to-all-start.1 = ((f32[16,384,128]{2,1,0:T(8,128)}), f32[16,384,128]{2,1,0:T(8,128)S(1)}, u32[]{:S(2)}, u32[]{:S(2)}) async-start(f32[16,384,128]{2,1,0:T(8,128)} %pack2.1), calls=%async_computation.1 | async-start | bytes 6291456 | tf_op jit(solution)/shard_map/all_to_all | solution.py:664
  67.9 0.7 slice_subtract_fusion
  68.5 19.0 %physical1.1 = (f32[16,128,128]{2,1,0:T(8,128)}, f32[16,128,128]{2,1,0:T(8,128)}, f32[8,128]{1,0:T(8,128)}) custom-call(s32[4096]{0:T(1024)} %bitcast.44, f32[16,256,128]{2,1,0:T(8,128)} %copy-done.3, bf16[512,256]{1,0:T(8,128)(2,1)} %constant.123.clone.high_ref, bf16[512,256]{1,0:T(8,128)(2,1)} %constant.124.clone.low_ref), custom_call_target="tpu_custom_call" | custom-call | flops 15000000512 | bytes 45000000 | tf_op jit(solution)/shard_map/physical1/pallas_call | solution.py:670
  87.6 0.4 collective-permute-start
  88.0 0.1 dynamic-slice_bitcast_fusion
  88.2 0.8 broadcast_multiply_fusion.1
  89.0 1.1 mul.101
  90.2 0.2 mul.104
  90.4 0.8 compare_reduce_fusion
  91.2 1.3 fusion.6.pos_ref
  92.6 18.1 %force1.1 = f32[16,264,128]{2,1,0:T(8,128)} custom-call(s32[4096]{0:T(1024)} %fusion.6.pos_ref, f32[16,128,128]{2,1,0:T(8,128)} %get-tuple-element.19.flow_ref.field_ref, f32[16,128,128]{2,1,0:T(8,128)} %get-tuple-element.19.flow_ref.field_ref, f32[16,128,128]{2,1,0:T(8,128)} %collective-permute-done.other_ref, f32[16,128,128]{2,1,0:T(8,128)} %get-tuple-element.20.span_ref, ...), custom_call_target="tpu_custom_call" | custom-call | flops 10000000000 | bytes 30000000 | tf_op jit(solution)/shard_map/force1/pallas_call | solution.py:690
  110.7 27.1 %all-to-all-done.1.in_ref = f32[16,384,128]{2,1,0:T(8,128)S(1)} async-done(((f32[16,384,128]{2,1,0:T(8,128)}), f32[16,384,128]{2,1,0:T(8,128)S(1)}, u32[]{:S(2)}, u32[]{:S(2)}) %all-to-all-start.1) | async-done | bytes 3145760 | tf_op jit(solution)/shard_map/all_to_all | solution.py:664
  137.8 1.7 copy-done.2
  139.4 4.9 %all-to-all-start.2 = ((f32[16,264,128]{2,1,0:T(8,128)}), f32[16,264,128]{2,1,0:T(8,128)S(1)}, u32[]{:S(2)}, u32[]{:S(2)}) async-start(f32[16,264,128]{2,1,0:T(8,128)} %force1.1), calls=%async_computation.2 | async-start | bytes 4325376 | tf_op jit(solution)/shard_map/all_to_all | solution.py:664
  144.3 42.9 %physical2.1 = (f32[24,128,128]{2,1,0:T(8,128)}, f32[24,128,128]{2,1,0:T(8,128)}, f32[8,128]{1,0:T(8,128)}) custom-call(s32[4096]{0:T(1024)} %bitcast.45, f32[16,384,128]{2,1,0:T(8,128)} %copy-done.2, bf16[512,256]{1,0:T(8,128)(2,1)} %constant.123.clone.high_ref, bf16[512,256]{1,0:T(8,128)(2,1)} %constant.124.clone.low_ref), custom_call_target="tpu_custom_call" | custom-call | flops 30000001024 | bytes 90000000 | tf_op jit(solution)/shard_map/physical2/pallas_call | solution.py:670
  187.3 0.3 collective-permute-start.1
  187.6 3.3 %collective-permute-done.1.other_ref = f32[24,128,128]{2,1,0:T(8,128)S(1)} collective-permute-done((f32[24,128,128]{2,1,0:T(8,128)}, f32[24,128,128]{2,1,0:T(8,128)S(1)}, u32[]{:S(2)}, u32[]{:S(2)}) %collective-permute-start.1) | collective-permute-done | bytes 1572896 | tf_op jit(solution)/shard_map/ppermute | solution.py:686
  190.9 1.2 copy-done.11
  192.1 23.0 %force2.1 = f32[16,384,128]{2,1,0:T(8,128)} custom-call(s32[4096]{0:T(1024)} %fusion.6.pos_ref, f32[16,128,128]{2,1,0:T(8,128)} %get-tuple-element.19.flow_ref.field_ref, f32[24,128,128]{2,1,0:T(8,128)} %get-tuple-element.24.field_ref, f32[24,128,128]{2,1,0:T(8,128)} %copy-done.11, f32[24,128,128]{2,1,0:T(8,128)} %get-tuple-element.25.span_ref, ...), custom_call_target="tpu_custom_call" | custom-call | flops 20000000000 | bytes 60000000 | tf_op jit(solution)/shard_map/force2/pallas_call | solution.py:690
  215.1 1.4 copy-done.1
  216.5 6.0 %all-to-all-start.3 = ((f32[16,384,128]{2,1,0:T(8,128)}), f32[16,384,128]{2,1,0:T(8,128)S(1)}, u32[]{:S(2)}, u32[]{:S(2)}) async-start(f32[16,384,128]{2,1,0:T(8,128)} %force2.1), calls=%async_computation.3 | async-start | bytes 6291456 | tf_op jit(solution)/shard_map/all_to_all | solution.py:664
  222.5 0.8 constant_dynamic-slice_fusion
  223.4 0.1 copy.25
  223.5 0.8 copy.26
  224.3 0.9 mul.108
  225.3 1.4 mul.109
  226.6 1.8 copy.21
  228.4 2.1 mul.106
  230.6 2.6 mul.107
  233.2 0.6 scatter_custom_fusion
  233.8 0.7 fusion.23
  234.5 4.4 %compare_select_fusion.10 = s32[512,1]{0,1:T(1,128)S(1)} fusion(s32[]{:T(128)} %bitcast.14, s32[]{:T(128)} %bitcast.15, s32[]{:T(128)} %bitcast.16, s32[]{:T(128)} %bitcast.17, s32[]{:T(128)} %bitcast.18, s32[]{:T(128)} %bitcast.20, s32[]{:T(128)} %bitcast.19), kind=kLoop, calls=%fused_computation.34 | loop fusion | flops 11776 | bytes 2076 | tf_op jit(solution)/shard_map/gather | solution.py:98
  238.9 0.7 fusion.22
  239.6 0.5 add_minimum_fusion
  240.2 0.6 convert_compare_fusion
  240.7 4.4 %compare_select_fusion.4 = s32[512,1]{0,1:T(1,128)S(1)} fusion(s32[]{:T(128)} %bitcast.23, s32[]{:T(128)} %bitcast.24, s32[]{:T(128)} %bitcast.25, s32[]{:T(128)} %bitcast.26, s32[]{:T(128)} %bitcast.27, s32[]{:T(128)} %bitcast.29, s32[]{:T(128)} %bitcast.28, s32[512,1]{0,1:T(1,128)S(1)} %bitcast.53), kind=kLoop, calls=%fused_computation.27 | loop fusion | flops 7680 | bytes 4124 | tf_op jit(solution)/shard_map/gather | solution.py:100
  245.1 5.6 %fusion.8 = s32[512]{0:T(512)S(1)} fusion(pred[512]{0:T(512)(128)(4,1)S(1)} %get-tuple-element.29, pred[512]{0:T(512)(128)(4,1)S(1)} %get-tuple-element.28, pred[512]{0:T(512)(128)(4,1)S(1)} %compare_reduce_fusion.1, s32[512]{0:T(512)S(1)} %bitcast.54, s32[]{:T(128)} %bitcast.29, s32[]{:T(128)} %bitcast.22, s32[]{:T(128)} %bitcast.23, s32[]{:T(128)} %bitcast.24, ...), kind=kLoop, calls=%fused_computation.50 | loop fusion | flops 11776 | bytes 8228 | tf_op jit(solution)/shard_map/jit(_where)/select_n | solution.py:103
  250.7 1.0 fusion.1.rim_ref
  251.7 1.7 compare_select_fusion.1
  253.4 1.9 broadcast_multiply_fusion.inverse_ref
  255.3 37.1 %all-to-all-done.3.second_ref = f32[16,384,128]{2,1,0:T(8,128)S(1)} async-done(((f32[16,384,128]{2,1,0:T(8,128)}), f32[16,384,128]{2,1,0:T(8,128)S(1)}, u32[]{:S(2)}, u32[]{:S(2)}) %all-to-all-start.3) | async-done | bytes 3145760 | tf_op jit(solution)/shard_map/all_to_all | solution.py:664
  292.4 1.6 copy-done
  294.1 29.6 %sweeps.1 = f32[10240,128]{1,0:T(8,128)} custom-call(f32[10240,128]{1,0:T(8,128)} %bitcast.42, f32[16,264,128]{2,1,0:T(8,128)} %copy-done.1, f32[16,384,128]{2,1,0:T(8,128)} %copy-done, f32[1,512]{1,0:T(1,128)} %bitcast.55, f32[25,512]{1,0:T(8,128)} %matrix_ref.1, f32[2,256,256]{2,1,0:T(8,128)} %broadcast_multiply_fusion.inverse_ref, ...), custom_call_target="tpu_custom_call" | custom-call | tf_op jit(solution)/shard_map/sweeps/pallas_call | solution.py:720
  (30 shorter events, 0.3 us)
Async XLA Ops:
  7.7 54.0 %all-to-all-start = ((f32[16,256,128]{2,1,0:T(8,128)}), f32[16,256,128]{2,1,0:T(8,128)S(1)}, u32[]{:S(2)}, u32[]{:S(2)}) async-start(f32[16,256,128]{2,1,0:T(8,128)} %pack1.1), calls=%async_computation | async-start | bytes 4194304 | tf_op jit(solution)/shard_map/all_to_all | solution.py:664
  21.9 46.0 %copy-start.4 = (s32[4096,2]{0,1:T(2,128)S(1)}, s32[4096,2]{0,1:T(2,128)}, u32[]{:S(2)}) copy-start(s32[4096,2]{0,1:T(2,128)} %param.12) | copy-start | bytes 98308
  61.6 1.3 copy-start.3
  63.0 74.8 %all-to-all-start.1 = ((f32[16,384,128]{2,1,0:T(8,128)}), f32[16,384,128]{2,1,0:T(8,128)S(1)}, u32[]{:S(2)}, u32[]{:S(2)}) async-start(f32[16,384,128]{2,1,0:T(8,128)} %pack2.1), calls=%async_computation.1 | async-start | bytes 6291456 | tf_op jit(solution)/shard_map/all_to_all | solution.py:664
  68.5 19.4 %copy-start.7 = (f32[64,64]{1,0:T(8,128)S(1)}, f32[64,64]{1,0:T(8,128)}, u32[]{:S(2)}) copy-start(f32[64,64]{1,0:T(8,128)} %param.17) | copy-start | bytes 49156
  68.5 22.7 %copy-start.5 = (s32[4096,1]{0,1:T(1,128)S(1)}, s32[4096,1]{0,1:T(1,128)}, u32[]{:S(2)}) copy-start(s32[4096,1]{0,1:T(1,128)} %get-tuple-element.38) | copy-start | bytes 49156
  87.6 5.0 %collective-permute-start = (f32[16,128,128]{2,1,0:T(8,128)}, f32[16,128,128]{2,1,0:T(8,128)}, u32[]{:S(2)}, u32[]{:S(2)}) collective-permute-start(f32[16,128,128]{2,1,0:T(8,128)} %get-tuple-element.19.flow_ref.field_ref), channel_id=1, source_target_pairs={{0,1},{1,0},{2,3},{3,2},{4,5},{5,4},{6,7},{7,6},{8,9},{9,8},{10,11... | collective-permute-start | bytes 3145736 | tf_op jit(solution)/shard_map/ppermute | solution.py:686
  88.2 0.9 copy-start.9
  90.4 2.2 copy-start.6
  137.8 1.7 copy-start.2
  139.4 75.7 %all-to-all-start.2 = ((f32[16,264,128]{2,1,0:T(8,128)}), f32[16,264,128]{2,1,0:T(8,128)S(1)}, u32[]{:S(2)}, u32[]{:S(2)}) async-start(f32[16,264,128]{2,1,0:T(8,128)} %force1.1), calls=%async_computation.2 | async-start | bytes 4325376 | tf_op jit(solution)/shard_map/all_to_all | solution.py:664
  187.3 3.6 %collective-permute-start.1 = (f32[24,128,128]{2,1,0:T(8,128)}, f32[24,128,128]{2,1,0:T(8,128)S(1)}, u32[]{:S(2)}, u32[]{:S(2)}) collective-permute-start(f32[24,128,128]{2,1,0:T(8,128)} %get-tuple-element.24.field_ref), channel_id=1, source_target_pairs={{0,1},{1,0},{2,3},{3,2},{4,5},{5,4},{6,7},{7,6},{8,9},{9,8},{10,11... | collective-permute-start | bytes 4718600 | tf_op jit(solution)/shard_map/ppermute | solution.py:686
  190.9 1.2 copy-start.11
  215.1 9.2 %copy-start.10 = (f32[4,4]{1,0:T(4,128)S(1)}, f32[4,4]{1,0:T(4,128)}, u32[]{:S(2)}) copy-start(f32[4,4]{1,0:T(4,128)} %copy-done.9) | copy-start | bytes 196
  215.1 1.4 copy-start.1
  216.5 75.9 %all-to-all-start.3 = ((f32[16,384,128]{2,1,0:T(8,128)}), f32[16,384,128]{2,1,0:T(8,128)S(1)}, u32[]{:S(2)}, u32[]{:S(2)}) async-start(f32[16,384,128]{2,1,0:T(8,128)} %force2.1), calls=%async_computation.3 | async-start | bytes 6291456 | tf_op jit(solution)/shard_map/all_to_all | solution.py:664
  225.3 7.9 %copy-start.8 = (s32[8]{0:T(128)S(1)}, s32[8]{0:T(128)}, u32[]{:S(2)}) copy-start(s32[8]{0:T(128)} %param.13) | copy-start | bytes 100
  292.4 1.6 copy-start
